TPU v7x, 32 devices: a whole 2x2x4 slice. The times are simulated.
32 devices in a mesh: client: 8 (over z, core), param: 4 (over y, x).
Axes of the slice: x: 2, y: 2, z: 4, core: 2. Of those that a mesh axis runs over, the one named last changes fastest.
Arguments:
- inputs: bfloat16 [8, 384, 2304], P('client', None, 'param'), may hold values from -6 to 6
- targets: bfloat16 [8, 384, 2304], P('client', None, 'param'), may hold values from -35 to 35
- norm_gain: float32 [2304], replicated, may hold values from 0.1 to 1.9
- gate_weight: bfloat16 [2304, 4608], P(None, 'param'), may hold values from -0.125 to 0.125
- up_weight: bfloat16 [2304, 4608], P(None, 'param'), may hold values from -0.125 to 0.125
- down_weight: bfloat16 [4608, 2304], P('param'), may hold values from -0.09375 to 0.09375
- neighbours: int32 [8], replicated, may hold values from 3 to 6
Outputs:
- update_gate: float32 [2304, 4608], P('client', 'param')
- update_up: float32 [2304, 4608], P('client', 'param')
- update_down: float32 [2304, 4608], P('client', 'param')
- relative_weight: float32 [8], replicated
All inputs are finite; a program needn't handle non-finite values.
Results may differ from a plain program's by a relative error of at most 0.0095.
Values may be sent and summed in bfloat16 or wider, within the bound.
A program may use at most 128 MiB of HBM per device.

v0:
```python
import math

import jax
import jax.numpy as jnp
from jax import lax
from jax.sharding import PartitionSpec as P


def gelu_tanh(values):
    return jax.nn.gelu(values, approximate=True)


def rms_normed(gathered, norm_gain):
    widened = gathered.astype(jnp.float32)
    inverse_rms = lax.rsqrt(jnp.mean(widened * widened, axis=-1, keepdims=True) + 1e-06)
    return (widened * inverse_rms * norm_gain).astype(jnp.bfloat16)


def krum_weights(gram, neighbours):
    client_count = gram.shape[0]
    diagonal = jnp.diagonal(gram)
    distance = diagonal[:, None] + diagonal[None, :] - 2.0 * gram
    row_index = lax.broadcasted_iota(jnp.int32, (client_count, client_count), 0)
    col_index = lax.broadcasted_iota(jnp.int32, (client_count, client_count), 1)
    distance = jnp.where(row_index == col_index, jnp.asarray(1e30, gram.dtype), distance)
    ordered = jnp.sort(distance, axis=1)
    scores = jnp.sum(
        jnp.where(col_index < neighbours[:, None], ordered, jnp.zeros_like(ordered)), axis=1
    )
    scaled = scores / jnp.mean(scores)
    exponent = jnp.exp(-4.0 * scaled)
    return exponent / jnp.sum(exponent)


def token_contract(left, right):
    return lax.dot_general(
        left, right, (((0,), (0,)), ((), ())), preferred_element_type=jnp.float32
    )


def pair_products(exchanged):
    flattened = exchanged.reshape(exchanged.shape[0], -1)
    return lax.dot_general(
        flattened, flattened, (((1,), (1,)), ((), ())), preferred_element_type=jnp.float32
    )


def weighted_sum(weights, exchanged):
    return jnp.sum(weights[:, None, None] * exchanged.astype(jnp.float32), axis=0)


def on_device(inputs, targets, norm_gain, gate_weight, up_weight, down_weight, neighbours):
    token_count = inputs.shape[1]
    factor = 1.0 / math.sqrt(token_count)
    gathered = lax.all_gather(inputs, "param", axis=2, tiled=True)
    normed = rms_normed(gathered[0], norm_gain)
    gate_value = jnp.dot(normed, gate_weight, preferred_element_type=jnp.float32)
    up_value = jnp.dot(normed, up_weight, preferred_element_type=jnp.float32)
    activated, gelu_back = jax.vjp(gelu_tanh, gate_value)
    hidden = (activated * up_value).astype(jnp.bfloat16)
    partial_out = jnp.dot(hidden, down_weight, preferred_element_type=jnp.float32)
    out_share = lax.psum_scatter(
        partial_out.astype(jnp.bfloat16), "param", scatter_dimension=1, tiled=True
    ).astype(jnp.float32)
    local_residual = ((out_share - targets[0].astype(jnp.float32)) * factor).astype(jnp.bfloat16)
    residual = lax.all_gather(local_residual, "param", axis=1, tiled=True)
    down_delta = (-token_contract(residual, hidden)).astype(jnp.bfloat16)
    back_hidden = lax.dot_general(
        residual, down_weight, (((1,), (1,)), ((), ())), preferred_element_type=jnp.float32
    )
    back_gate = gelu_back(back_hidden * up_value)[0].astype(jnp.bfloat16)
    back_up = (back_hidden * activated).astype(jnp.bfloat16)
    gate_delta = (-token_contract(normed, back_gate)).astype(jnp.bfloat16)
    up_delta = (-token_contract(normed, back_up)).astype(jnp.bfloat16)
    owned_gate, owned_up, owned_down = (
        lax.all_to_all(gate_delta[None], "client", split_axis=1, concat_axis=0, tiled=True),
        lax.all_to_all(up_delta[None], "client", split_axis=1, concat_axis=0, tiled=True),
        lax.all_to_all(down_delta[None], "client", split_axis=1, concat_axis=0, tiled=True),
    )
    partial_gram = pair_products(owned_gate) + pair_products(owned_up) + pair_products(owned_down)
    gram = lax.psum(partial_gram, ("client", "param"))
    weights = krum_weights(gram, neighbours)
    client_count = lax.axis_size("client")
    update_gate = weighted_sum(weights, owned_gate)
    update_up = weighted_sum(weights, owned_up)
    update_down = weighted_sum(weights, owned_down)
    return (update_gate, update_up, update_down, client_count * weights)


def solution(mesh):
    in_specs = (
        P("client", None, "param"),
        P("client", None, "param"),
        P(),
        P(None, "param"),
        P(None, "param"),
        P("param", None),
        P(),
    )
    out_specs = (P("client", "param"), P("client", "param"), P("client", "param"), P())
    return jax.shard_map(
        on_device, mesh=mesh, in_specs=in_specs, out_specs=out_specs, check_vma=False
    )
```

profile of v0, /device:TPU:0, one launch (start us, length us, event | category | flops | bytes accessed | tf_op | source)
XLA Modules:
  0.0 661.1 jit_solution(12254492305483622144)
XLA Ops:
  7.2 0.7 all-gather.3.cloned.1.call-update
  8.0 37.2 %all-gather.3.cloned.1.call-done = bf16[1,384,2304]{1,2,0:T(8,128)(2,1)} async-done(((bf16[1,384,576]{1,2,0:T(8,128)(2,1)}), bf16[1,384,2304]{1,2,0:T(8,128)(2,1)}) %all-gather.3.cloned.1.call-update) | async-done | bytes 1769488 | tf_op jit(solution)/shard_map/all_gather | solution.py:55
  45.2 2.1 fusion.12
  47.3 5.3 fusion.63
  52.7 4.3 multiply_convert_fusion.1
  57.1 4.4 convolution_convert_fusion
  61.5 0.2 all-gather.5.cloned.1.call-start
  61.7 32.4 %reduce-scatter.2.cloned.1.call-done = bf16[384,576]{0,1:T(8,128)(2,1)} async-done(((bf16[384,2304]{0,1:T(8,128)(2,1)}), bf16[384,576]{0,1:T(8,128)(2,1)}) %reduce-scatter.2.cloned.1.call-update) | async-done | bytes 442384 | tf_op jit(solution)/shard_map/reduce_scatter | solution.py:62
  94.2 1.9 fusion.39
  96.1 33.1 %all-gather.5.cloned.1.call-done = bf16[384,2304]{0,1:T(8,128)(2,1)} async-done(((bf16[384,576]{0,1:T(8,128)(2,1)}), bf16[384,2304]{0,1:T(8,128)(2,1)}) %all-gather.5.cloned.1.call-update) | async-done | bytes 1769488 | tf_op jit(solution)/shard_map/all_gather | solution.py:66
  129.2 5.7 fusion.66
  134.9 3.6 fusion.5
  138.5 35.3 %copy.62 = bf16[1,2304,1152]{2,0,1:T(2,128)(2,1)} copy(bf16[1,2304,1152]{2,1,0:T(8,128)(2,1)S(1)} %fusion.5) | data formatting | bytes 10616832 | tf_op jit(solution)/shard_map/broadcast_in_dim | solution.py:76
  173.8 0.5 broadcast.143
  174.3 33.8 %reduce.2 = bf16[2304,1152]{1,0:T(8,128)(2,1)} reduce(bf16[2304,1,1152]{2,1,0:T(2,128)(2,1)} %bitcast.54, bf16[]{:T(256)} %broadcast.143), dimensions={1}, to_apply=%bitcast.53.reduce_sub_computation | reduce | bytes 10616834
  208.1 7.6 %reshape.91 = bf16[8,2,165888]{2,1,0:T(2,128)(2,1)} reshape(bf16[2304,1152]{1,0:T(8,128)(2,1)} %reduce.2) | data formatting | bytes 10616832
  215.7 5.1 all-to-all-start
  220.8 5.9 fusion.4
  226.7 35.3 %copy.61 = bf16[1,2304,1152]{2,0,1:T(2,128)(2,1)} copy(bf16[1,2304,1152]{2,1,0:T(8,128)(2,1)S(1)} %fusion.4) | data formatting | bytes 10616832 | tf_op jit(solution)/shard_map/broadcast_in_dim | solution.py:77
  261.9 33.8 %reduce.3 = bf16[2304,1152]{1,0:T(8,128)(2,1)} reduce(bf16[2304,1,1152]{2,1,0:T(2,128)(2,1)} %bitcast.56, bf16[]{:T(256)} %broadcast.143), dimensions={1}, to_apply=%bitcast.52.reduce_sub_computation | reduce | bytes 10616834
  295.7 7.7 %reshape.93 = bf16[8,2,165888]{2,1,0:T(2,128)(2,1)} reshape(bf16[2304,1152]{1,0:T(8,128)(2,1)} %reduce.3) | data formatting | bytes 10616832
  303.4 35.3 %all-to-all-done = bf16[8,2,165888]{2,1,0:T(2,128)(2,1)} async-done(((bf16[8,2,165888]{2,1,0:T(2,128)(2,1)}), bf16[8,2,165888]{2,1,0:T(2,128)(2,1)}, u32[]{:S(2)}, u32[]{:S(2)}) %all-to-all-start) | async-done | bytes 5308448 | tf_op jit(solution)/shard_map/all_to_all | solution.py:76
  338.7 4.7 all-to-all-start.1
  343.4 3.3 fusion.3
  346.6 35.3 %copy.60 = bf16[1,2304,1152]{2,0,1:T(2,128)(2,1)} copy(bf16[1,2304,1152]{2,1,0:T(8,128)(2,1)S(1)} %fusion.3) | data formatting | bytes 10616832 | tf_op jit(solution)/shard_map/broadcast_in_dim | solution.py:78
  381.9 33.7 %reduce.1 = bf16[2304,1152]{1,0:T(8,128)(2,1)} reduce(bf16[2304,1,1152]{2,1,0:T(2,128)(2,1)} %bitcast.55, bf16[]{:T(256)} %broadcast.143), dimensions={1}, to_apply=%bitcast.51.reduce_sub_computation | reduce | bytes 10616834
  415.6 7.7 %reshape.89 = bf16[8,2,165888]{2,1,0:T(2,128)(2,1)} reshape(bf16[2304,1152]{1,0:T(8,128)(2,1)} %reduce.1) | data formatting | bytes 10616832
  423.3 38.0 %all-to-all-done.1 = bf16[8,2,165888]{2,1,0:T(2,128)(2,1)} async-done(((bf16[8,2,165888]{2,1,0:T(2,128)(2,1)}), bf16[8,2,165888]{2,1,0:T(2,128)(2,1)}, u32[]{:S(2)}, u32[]{:S(2)}) %all-to-all-start.1) | async-done | bytes 5308448 | tf_op jit(solution)/shard_map/all_to_all | solution.py:77
  461.2 4.8 all-to-all-start.2
  466.1 9.8 %reshape.92 = bf16[2304,1,1152]{2,1,0:T(2,128)(2,1)} reshape(bf16[8,2,165888]{2,1,0:T(2,128)(2,1)} %all-to-all-done) | data formatting | bytes 10616832
  475.9 7.3 %copy.38 = bf16[1,2304,1152]{2,1,0:T(8,128)(2,1)} copy(bf16[1,2304,1152]{2,0,1:T(2,128)(2,1)} %bitcast.57) | data formatting | bytes 10616832
  483.2 9.9 %reshape.94 = bf16[2304,1,1152]{2,1,0:T(2,128)(2,1)} reshape(bf16[8,2,165888]{2,1,0:T(2,128)(2,1)} %all-to-all-done.1) | data formatting | bytes 10616832
  493.1 7.3 %copy.39 = bf16[1,2304,1152]{2,1,0:T(8,128)(2,1)} copy(bf16[1,2304,1152]{2,0,1:T(2,128)(2,1)} %bitcast.58) | data formatting | bytes 10616832
  500.5 3.9 fusion.22
  504.3 79.6 %all-to-all-done.2 = bf16[8,2,165888]{2,1,0:T(2,128)(2,1)} async-done(((bf16[8,2,165888]{2,1,0:T(2,128)(2,1)}), bf16[8,2,165888]{2,1,0:T(2,128)(2,1)}, u32[]{:S(2)}, u32[]{:S(2)}) %all-to-all-start.2) | async-done | bytes 5308448 | tf_op jit(solution)/shard_map/all_to_all | solution.py:78
  584.0 9.9 %reshape.90 = bf16[2304,1,1152]{2,1,0:T(2,128)(2,1)} reshape(bf16[8,2,165888]{2,1,0:T(2,128)(2,1)} %all-to-all-done.2) | data formatting | bytes 10616832
  593.9 5.0 copy.40
  599.0 0.1 slice-done.3
  599.1 2.1 fusion.34
  601.2 0.1 copy-done
  601.2 2.1 fusion.31
  603.3 36.9 %psum.7 = f32[8,8]{1,0:T(8,128)S(1)} all-reduce(f32[8,8]{1,0:T(8,128)S(1)} %fusion.31), channel_id=1, replica_groups=mesh['client'=8,'param'=4] {'client','param'}, use_global_device_ids=true, to_apply=%region_2.0 | all-reduce | flops 64 | bytes 512 | tf_op jit(solution)/shard_map/psum | solution.py:81
  640.2 0.6 gather_fusion
  641.0 0.7 sort.15
  641.7 0.6 fusion.47
  642.9 0.6 fusion.65
  643.6 1.2 broadcast_multiply_fusion
  644.7 9.7 %multiply_reduce_fusion = (f32[288,1152]{1,0:T(8,128)}, f32[288,1152]{1,0:T(8,128)}, f32[288,1152]{1,0:T(8,128)}) fusion(bf16[8,288,1152]{2,1,0:T(8,128)(2,1)} %bitcast.69, f32[8]{0:T(128)S(1)} %get-tuple-element.13, bf16[8,288,1152]{2,1,0:T(8,128)(2,1)} %bitcast.64, bf16[8,288,1152]{2,1,0:T(8,128)(2,1)} %bitcast.60), kind=kLoop, calls=%fused_computation.7 | loop fusion | flops 22892544 | bytes 19906592 | tf_op jit(solution)/shard_map/reduce_sum | solution.py:49
  (47 shorter events, 0.4 us)
Async XLA Ops:
  7.2 40.1 %copy-start.5 = (f32[2304]{0:T(1024)S(1)}, f32[2304]{0:T(1024)}, u32[]{:S(2)}) copy-start(f32[2304]{0:T(1024)} %param.9) | copy-start | bytes 27652
  7.2 38.0 %all-gather.3.cloned.1.call-start = ((), (), s32[]{:S(2)}) async-start(), calls=%async_computation.4 | async-start | bytes 2211840 | tf_op jit(solution)/shard_map/all_gather | solution.py:55
  7.9 86.2 %reduce-scatter.2.cloned.1.call-start = ((), (), s32[]{:S(2)}) async-start(), calls=%async_computation.5 | async-start | bytes 2211840 | tf_op jit(solution)/shard_map/reduce_scatter | solution.py:62
  45.2 2.1 copy-start.1
  45.2 7.5 %slice-start.4 = ((s8[5308416]{0:T(1024)(128)(4,1)}), s8[4194304]{0:T(1024)(128)(4,1)S(1)}, s32[]{:S(2)}) async-start(s8[5308416]{0:T(1024)(128)(4,1)} %bitcast.70), calls=%async_computation.11 | async-start | bytes 8388608
  47.3 5.4 slice-start.5
  47.3 9.8 %slice-start.6 = ((s8[5308416]{0:T(1024)(128)(4,1)}), s8[4194304]{0:T(1024)(128)(4,1)S(1)}, s32[]{:S(2)}) async-start(s8[5308416]{0:T(1024)(128)(4,1)} %bitcast.72), calls=%async_computation.13 | async-start | bytes 8388608
  52.7 4.4 copy-start.6
  52.7 4.4 slice-start.7
  61.5 32.7 %copy-start.2 = (bf16[1,384,576]{1,2,0:T(8,128)(2,1)S(1)}, bf16[1,384,576]{1,2,0:T(8,128)(2,1)}, u32[]{:S(2)}) copy-start(bf16[1,384,576]{1,2,0:T(8,128)(2,1)} %param.8) | copy-start | bytes 1327108
  61.5 67.7 %all-gather.5.cloned.1.call-start = ((), (), s32[]{:S(2)}) async-start(), calls=%async_computation.6 | async-start | bytes 2211840 | tf_op jit(solution)/shard_map/all_gather | solution.py:66
  129.2 5.7 copy-start.7
  129.2 5.7 copy-start.8
  134.9 3.6 copy-start.9
  215.7 123.0 %all-to-all-start = ((bf16[8,2,165888]{2,1,0:T(2,128)(2,1)}), bf16[8,2,165888]{2,1,0:T(2,128)(2,1)}, u32[]{:S(2)}, u32[]{:S(2)}) async-start(bf16[8,2,165888]{2,1,0:T(2,128)(2,1)} %reshape.91), calls=%async_computation.1 | async-start | bytes 10616832 | tf_op jit(solution)/shard_map/all_to_all | solution.py:76
  303.4 40.0 %copy-start.4 = (bf16[384,2304]{0,1:T(8,128)(2,1)S(1)}, bf16[384,2304]{0,1:T(8,128)(2,1)}, u32[]{:S(2)}) copy-start(bf16[384,2304]{0,1:T(8,128)(2,1)} %all-gather.5.cloned.1.call-done) | copy-start | bytes 5308420
  338.7 122.6 %all-to-all-start.1 = ((bf16[8,2,165888]{2,1,0:T(2,128)(2,1)}), bf16[8,2,165888]{2,1,0:T(2,128)(2,1)}, u32[]{:S(2)}, u32[]{:S(2)}) async-start(bf16[8,2,165888]{2,1,0:T(2,128)(2,1)} %reshape.93), calls=%async_computation.2 | async-start | bytes 10616832 | tf_op jit(solution)/shard_map/all_to_all | solution.py:77
  461.2 122.7 %all-to-all-start.2 = ((bf16[8,2,165888]{2,1,0:T(2,128)(2,1)}), bf16[8,2,165888]{2,1,0:T(2,128)(2,1)}, u32[]{:S(2)}, u32[]{:S(2)}) async-start(bf16[8,2,165888]{2,1,0:T(2,128)(2,1)} %reshape.89), calls=%async_computation.3 | async-start | bytes 10616832 | tf_op jit(solution)/shard_map/all_to_all | solution.py:78
  483.2 17.3 %slice-start = ((s8[5308416]{0:T(1024)(128)(4,1)}), s8[1114112]{0:T(1024)(128)(4,1)S(1)}, s32[]{:S(2)}) async-start(s8[5308416]{0:T(1024)(128)(4,1)} %bitcast.61), calls=%async_computation.7 | async-start | bytes 2228224
  493.1 7.3 %slice-start.1 = ((s8[5308416]{0:T(1024)(128)(4,1)}), s8[4194304]{0:T(1024)(128)(4,1)S(1)}, s32[]{:S(2)}) async-start(s8[5308416]{0:T(1024)(128)(4,1)} %bitcast.61), calls=%async_computation.8 | async-start | bytes 8388608
  584.0 15.0 %slice-start.2 = ((s8[5308416]{0:T(1024)(128)(4,1)}), s8[1114112]{0:T(1024)(128)(4,1)S(1)}, s32[]{:S(2)}) async-start(s8[5308416]{0:T(1024)(128)(4,1)} %bitcast.65), calls=%async_computation.9 | async-start | bytes 2228224
  593.9 5.2 slice-start.3
  598.9 2.3 copy-start
  601.2 40.4 %copy-start.3 = (s32[8]{0:T(128)S(1)}, s32[8]{0:T(128)}, u32[]{:S(2)}) copy-start(s32[8]{0:T(128)} %param.13) | copy-start | bytes 100
Sparse Core Ops, SparseCore 0:
  9.8 35.2 all-gather.2
  61.6 32.4 reduce-scatter.1
  96.6 32.5 all-gather.4
where the time goes:
time: 669 us; the launch traced here: 661 us
  waiting for transfers between devices  256 us (38%)
  local copies, waits for them, and re-layouts  180 us (27%)
  other arithmetic  118 us (18%)
  matrix products  40.5 us (6%)
  blocking collectives  36.9 us (6%)
  starting transfers between devices  14.9 us (2%)
  between operations  14.8 us (2%)
    unnamed x7, other arithmetic  101 us
    all_to_all x1, waiting for transfers between devices, on_device(): lax.all_to_all(down_delta[None], 'client', split_axis=1, concat_axis=0, t...  79.6 us
    unnamed x46, local copies, waits for them, and re-layouts  73.1 us
    all_to_all x1, waiting for transfers between devices, on_device(): lax.all_to_all(up_delta[None], 'client', split_axis=1, concat_axis=0, til...  38 us
    all_gather x1, waiting for transfers between devices, on_device(): gathered = lax.all_gather(inputs, 'param', axis=2, tiled=True)  37.2 us
    psum x1, blocking collectives, on_device(): gram = lax.psum(partial_gram, ('client', 'param'))  36.9 us
    all_to_all x1, waiting for transfers between devices, on_device(): lax.all_to_all(gate_delta[None], 'client', split_axis=1, concat_axis=0, t...  35.3 us
    broadcast_in_dim x1, local copies, waits for them, and re-layouts, on_device(): gate_delta[None]  35.3 us
  transfers between devices with their start and end apart: 6, of which 6 were waited for; matrix products, arithmetic and copies ran while one was open for 30% of the time, Pallas kernels for 0%

commit v1 on v0

--- a/solution.py
+++ b/solution.py
@@ -1,8 +1,11 @@
+import functools
 import math
 
 import jax
 import jax.numpy as jnp
 from jax import lax
+from jax.experimental import pallas as pl
+from jax.experimental.pallas import tpu as pltpu
 from jax.sharding import PartitionSpec as P
 
 
@@ -86,6 +89,165 @@
     update_down = weighted_sum(weights, owned_down)
     return (update_gate, update_up, update_down, client_count * weights)
 
+PAIR = 2
+
+
+def delta_gram_kernel(left_ref, right_ref, delta_ref, gram_ref, totals):
+    clients, rows, columns = delta_ref.shape
+
+    @pl.when((pl.program_id(0) == 0) & (pl.program_id(1) == 0))
+    def _():
+        totals[...] = jnp.zeros_like(totals)
+
+    for client in range(clients):
+        product = jnp.dot(left_ref[client], right_ref[client], preferred_element_type=jnp.float32)
+        delta_ref[client] = (-product).astype(jnp.bfloat16)
+
+    pairs = [(i, j) for i in range(clients) for j in range(i, clients)]
+    lanes = columns // 128 * 128
+    tail = columns - lanes
+
+    def accumulate(row, at, width, sums):
+        tiles = [
+            delta_ref[client, pl.ds(row, 16), at : at + width].astype(jnp.float32)
+            for client in range(clients)
+        ]
+        found = []
+        for (i, j), total in zip(pairs, sums):
+            product = tiles[i] * tiles[j]
+            found.append(total + (product[:8] + product[8:]))
+        return tuple(found)
+
+    def step(index, sums):
+        row = pl.multiple_of(index * 16, 16)
+        for at in range(0, lanes, 128):
+            sums = accumulate(row, at, 128, sums)
+        return sums
+
+    zeros = tuple(jnp.zeros((8, 128), jnp.float32) for _ in pairs)
+    sums = lax.fori_loop(0, rows // 16, step, zeros)
+    for at, total in enumerate(sums):
+        totals[at] += total
+    if tail:
+
+        def tail_step(index, sums):
+            return accumulate(pl.multiple_of(index * 16, 16), lanes, tail, sums)
+
+        zeros = tuple(jnp.zeros((8, tail), jnp.float32) for _ in pairs)
+        sums = lax.fori_loop(0, rows // 16, tail_step, zeros)
+        for at, total in enumerate(sums):
+            totals[at, :, :tail] += total
+
+    last = (pl.program_id(0) == pl.num_programs(0) - 1) & (
+        pl.program_id(1) == pl.num_programs(1) - 1
+    )
+
+    @pl.when(last)
+    def _():
+        gram_ref[...] = jnp.sum(totals[...], axis=1)
+
+
+def deltas_and_gram(left, right):
+    _, clients, rows, tokens = left.shape
+    columns = right.shape[3]
+    row_tile = 96 if rows % 96 == 0 else rows
+    pair_count = clients * (clients + 1) // 2
+    deltas, sums = pl.pallas_call(
+        delta_gram_kernel,
+        grid=(3, rows // row_tile),
+        in_specs=[
+            pl.BlockSpec((None, clients, row_tile, tokens), lambda kind, at: (kind // 2, 0, at, 0)),
+            pl.BlockSpec((None, clients, tokens, columns), lambda kind, at: (kind, 0, 0, 0)),
+        ],
+        out_specs=[
+            pl.BlockSpec((None, clients, row_tile, columns), lambda kind, at: (kind, 0, at, 0)),
+            pl.BlockSpec((pair_count, 128), lambda kind, at: (0, 0)),
+        ],
+        out_shape=[
+            jax.ShapeDtypeStruct((3, clients, rows, columns), jnp.bfloat16),
+            jax.ShapeDtypeStruct((pair_count, 128), jnp.float32),
+        ],
+        scratch_shapes=[pltpu.VMEM((pair_count, 8, 128), jnp.float32)],
+        compiler_params=pltpu.CompilerParams(vmem_limit_bytes=48 * 2**20),
+        cost_estimate=pl.CostEstimate(
+            flops=6 * clients * rows * tokens * columns, bytes_accessed=40 * 2**20, transcendentals=0
+        ),
+        name="deltas_and_gram",
+    )(left, right)
+    upper = jnp.sum(sums, axis=1)
+    index = jnp.asarray([[place_count(clients, min(i, j), max(i, j)) for j in range(clients)] for i in range(clients)])
+    return deltas, upper[index]
+
+
+def place_count(clients, i, j):
+    return i * clients - i * (i - 1) // 2 + (j - i)
+
+
+def laid_out(gathered):
+    clients, params, tokens, width = gathered.shape
+    return gathered.transpose(0, 2, 1, 3).reshape(clients, tokens, params * width)
+
+
+def on_device_shared(inputs, targets, norm_gain, gate_weight, up_weight, down_weight, neighbours):
+    token_count = inputs.shape[1]
+    clients = lax.axis_size("client")
+    params = lax.axis_size("param")
+    client = lax.axis_index("client")
+    width = inputs.shape[2]
+    depth = width * params
+    core = client % PAIR
+    half = gate_weight.shape[1] // PAIR
+    chip_rows = depth // clients * PAIR
+    factor = 1.0 / math.sqrt(token_count)
+
+    own = lax.all_gather(inputs, "param", axis=2, tiled=True)[0]
+    every_input = lax.all_gather(inputs[0], ("client", "param"), axis=0)
+    normed_own = rms_normed(own, norm_gain)
+    gate_value = jnp.dot(normed_own, gate_weight, preferred_element_type=jnp.float32)
+    up_value = jnp.dot(normed_own, up_weight, preferred_element_type=jnp.float32)
+    hidden = (gelu_tanh(gate_value) * up_value).astype(jnp.bfloat16)
+    partial_out = jnp.dot(hidden, down_weight, preferred_element_type=jnp.float32)
+    out_share = lax.psum_scatter(
+        partial_out.astype(jnp.bfloat16), "param", scatter_dimension=1, tiled=True
+    ).astype(jnp.float32)
+    local_residual = ((out_share - targets[0].astype(jnp.float32)) * factor).astype(jnp.bfloat16)
+    every_residual = lax.all_gather(local_residual, ("client", "param"), axis=0)
+
+    gate_half = lax.dynamic_slice_in_dim(gate_weight, core * half, half, 1)
+    up_half = lax.dynamic_slice_in_dim(up_weight, core * half, half, 1)
+    down_half = lax.dynamic_slice_in_dim(down_weight, core * half, half, 0)
+    shape = (clients, params, token_count, width)
+    normed = rms_normed(laid_out(every_input.reshape(shape)), norm_gain)
+    residual = laid_out(every_residual.reshape(shape))
+    gate_value = jnp.dot(normed, gate_half, preferred_element_type=jnp.float32)
+    up_value = jnp.dot(normed, up_half, preferred_element_type=jnp.float32)
+    activated, gelu_back = jax.vjp(gelu_tanh, gate_value)
+    hidden = (activated * up_value).astype(jnp.bfloat16)
+    back_hidden = lax.dot_general(
+        residual, down_half, (((2,), (1,)), ((), ())), preferred_element_type=jnp.float32
+    )
+    back_gate = gelu_back(back_hidden * up_value)[0].astype(jnp.bfloat16)
+    back_up = (back_hidden * activated).astype(jnp.bfloat16)
+    rows_at = client // PAIR * chip_rows
+    left = jnp.stack(
+        [
+            lax.dynamic_slice_in_dim(array, rows_at, chip_rows, 2).transpose(0, 2, 1)
+            for array in (normed, residual)
+        ]
+    )
+    deltas, partial_gram = deltas_and_gram(left, jnp.stack([back_gate, back_up, hidden]))
+    gram = lax.psum(partial_gram, ("client", "param"))
+    weights = krum_weights(gram, neighbours)
+    updates = jnp.sum(weights[None, :, None, None] * deltas.astype(jnp.float32), axis=1)
+    updates = updates.reshape(3, PAIR, chip_rows // PAIR, half)
+    kept = lax.dynamic_index_in_dim(updates, core, 1, keepdims=False)
+    sent = lax.dynamic_index_in_dim(updates, 1 - core, 1, keepdims=False)
+    arrived = lax.ppermute(sent, "client", [(i, i ^ 1) for i in range(clients)])
+    first = jnp.where(core == 0, kept, arrived)
+    second = jnp.where(core == 0, arrived, kept)
+    whole = jnp.concatenate([first, second], axis=2)
+    return (whole[0], whole[1], whole[2], clients * weights)
+
 
 def solution(mesh):
     in_specs = (
@@ -98,6 +260,8 @@
         P(),
     )
     out_specs = (P("client", "param"), P("client", "param"), P("client", "param"), P())
+    shared = mesh.shape["client"] <= 8 and mesh.shape["client"] % PAIR == 0
+    body = on_device_shared if shared else on_device
     return jax.shard_map(
-        on_device, mesh=mesh, in_specs=in_specs, out_specs=out_specs, check_vma=False
-    )
+        body, mesh=mesh, in_specs=in_specs, out_specs=out_specs, check_vma=False
+    )

time: 669 us -> 514 us (0.77)
  local copies, waits for them, and re-layouts: 180 us -> 67.8 us
  other arithmetic: 118 us -> 63.9 us
  waiting for transfers between devices: 256 us -> 206 us
  Pallas kernels: 0 us -> 36.8 us
  matrix products: 40.5 us -> 74.6 us
  starting transfers between devices: 14.9 us -> 0.33 us
    all_to_all x3 -> x0, waiting for transfers between devices: 153 us -> none  [the longest x1 79.6 us: on_device(): lax.all_to_all(down_delta[None], 'client', split_axis=1, concat_axis=0, t...]
    broadcast_in_dim x3 -> x0, local copies, waits for them, and re-layouts: 106 us -> none  [the longest x1 35.3 us: on_device(): gate_delta[None]]
    unnamed x7 -> x1, other arithmetic: 101 us -> 0.01 us
    all_gather x2 -> x3, waiting for transfers between devices: 70.3 us -> 166 us  [the longest x1 70.4 us: on_device_shared(): every_input = lax.all_gather(inputs[0], ('client', 'param'), axis=0)]
    unnamed x46 -> x18, local copies, waits for them, and re-layouts: 73.1 us -> 2.05 us
    pallas_call x0 -> x1, Pallas kernels: none -> 36.8 us  [deltas_and_gram(): pl.pallas_call(delta_gram_kernel, grid=(3, rows // row_tile), in_specs=[p...]
    dot_general x10 -> x5, matrix products: 40.5 us -> 74.6 us  [the longest x1 27.5 us: on_device_shared(): gate_value = jnp.dot(normed, gate_half, preferred_element_type=jnp.float32)]
    reshape x0 -> x2, local copies, waits for them, and re-layouts: none -> 31.1 us  [on_device_shared(): residual = laid_out(every_residual.reshape(shape))]
  transfers between devices with their start and end apart: 6 -> 5, of which waited for: 6 -> 5; matrix products, arithmetic and copies ran while one was open for 30% -> 10% of each run, Pallas kernels for 0% -> 0%
where the time goes in v1:
time: 514 us; the launch traced here: 505 us
  waiting for transfers between devices  206 us (40%)
  matrix products  74.6 us (15%)
  local copies, waits for them, and re-layouts  67.8 us (13%)
  other arithmetic  63.9 us (12%)
  blocking collectives  38.6 us (8%)
  Pallas kernels  36.8 us (7%)
  between operations  16.8 us (3%)
    all_gather x1, waiting for transfers between devices, on_device_shared(): every_input = lax.all_gather(inputs[0], ('client', 'param'), axis=0)  70.4 us
    all_gather x1, waiting for transfers between devices, on_device_shared(): every_residual = lax.all_gather(local_residual, ('client', 'param'), axis=0)  58.1 us
    psum x1, blocking collectives, on_device_shared(): gram = lax.psum(partial_gram, ('client', 'param'))  38.6 us
    all_gather x1, waiting for transfers between devices, on_device_shared(): own = lax.all_gather(inputs, 'param', axis=2, tiled=True)[0]  37.2 us
    pallas_call x1, Pallas kernels, deltas_and_gram(): pl.pallas_call(delta_gram_kernel, grid=(3, rows // row_tile), in_specs=[p...  36.8 us
    reduce_scatter x1, waiting for transfers between devices, on_device_shared(): lax.psum_scatter(partial_out.astype(jnp.bfloat16), 'param', scatter_dimen...  35 us
    reshape x2, local copies, waits for them, and re-layouts, on_device_shared(): residual = laid_out(every_residual.reshape(shape))  31.1 us
    dot_general x1, matrix products, on_device_shared(): gate_value = jnp.dot(normed, gate_half, preferred_element_type=jnp.float32)  27.5 us
  transfers between devices with their start and end apart: 5, of which 5 were waited for; matrix products, arithmetic and copies ran while one was open for 10% of the time, Pallas kernels for 0%

profile of v1, /device:TPU:0, one launch (start us, length us, event | category | flops | bytes accessed | tf_op | source)
XLA Modules:
  0.0 505.4 jit_solution(5501942930590425165)
XLA Ops:
  8.0 0.0 all-gather.7.cloned.1.call-start
  8.0 0.7 all-gather.7.cloned.1.call-update
  8.7 0.0 reduce-scatter.2.cloned.1.call-start
  8.8 37.2 %all-gather.7.cloned.1.call-done = bf16[1,384,2304]{1,2,0:T(8,128)(2,1)} async-done(((bf16[1,384,576]{1,2,0:T(8,128)(2,1)}), bf16[1,384,2304]{1,2,0:T(8,128)(2,1)}) %all-gather.7.cloned.1.call-update) | async-done | bytes 1769488 | tf_op jit(solution)/shard_map/all_gather | solution.py:203
  46.0 1.9 fusion.12
  48.0 7.0 %fusion.41 = f32[384,1152]{1,0:T(8,128)} fusion(bf16[2304,1152]{1,0:T(8,128)(2,1)} %param.11, bf16[1,384,2304]{1,2,0:T(8,128)(2,1)} %all-gather.7.cloned.1.call-done, f32[2304]{0:T(1024)} %param.10, f32[384]{0:T(512)S(1)} %add_rsqrt_fusion.1), kind=kOutput, calls=%fused_computation.67 | convolution fusion | flops 2041970688 | bytes 8858112 | tf_op jit(solution)/shard_map/dot_general | solution.py:206
  55.0 12.0 %convolution_convert_fusion = bf16[384,2304]{0,1:T(8,128)(2,1)} fusion(bf16[1152,2304]{1,0:T(8,128)(2,1)} %param.13, bf16[2304,1152]{1,0:T(8,128)(2,1)} %param.12, f32[384,1152]{1,0:T(8,128)} %fusion.41, bf16[1,384,2304]{1,2,0:T(8,128)(2,1)S(1)} %copy-done.2, f32[2304]{0:T(1024)S(1)} %copy-done.4, f32[384]{0:T(512)S(1)} %add_rsqrt_fusion.1), kind=kOutput, calls=%fused_computation.27 | convolution fusion | flops 4085710848 | bytes 15936000 | tf_op jit(solution)/shard_map/dot_general | solution.py:209
  67.1 0.0 all-gather.5.cloned.1.call-start
  67.1 0.5 all-gather.5.cloned.1.call-update
  67.7 0.2 all-gather.9.cloned.1.call-start
  67.9 35.0 %reduce-scatter.2.cloned.1.call-done = bf16[384,576]{0,1:T(8,128)(2,1)} async-done(((bf16[384,2304]{0,1:T(8,128)(2,1)}), bf16[384,576]{0,1:T(8,128)(2,1)}) %reduce-scatter.2.cloned.1.call-update) | async-done | bytes 442384 | tf_op jit(solution)/shard_map/reduce_scatter | solution.py:210
  102.9 1.9 fusion.38
  104.8 0.0 all-gather.9.cloned.1.call-update
  104.9 70.4 %all-gather.5.cloned.1.call-done = bf16[32,384,576]{1,2,0:T(8,128)(2,1)} async-done(((bf16[1,384,576]{1,2,0:T(8,128)(2,1)}), bf16[32,384,576]{1,2,0:T(8,128)(2,1)}) %all-gather.5.cloned.1.call-update) | async-done | bytes 14155792 | tf_op jit(solution)/shard_map/all_gather | solution.py:204
  175.3 7.8 %multiply_reduce_fusion.1 = f32[32,384]{1,0:T(8,128)S(1)} fusion(bf16[32,384,576]{1,2,0:T(8,128)(2,1)} %all-gather.5.cloned.1.call-done), kind=kLoop, calls=%fused_computation.6 | loop fusion | flops 21221376 | bytes 14204928 | tf_op jit(solution)/shard_map/reduce_sum | solution.py:18
  183.2 8.1 %convert_element_type.82 = f32[32,384,576]{1,2,0:T(8,128)S(1)} convert(bf16[32,384,576]{1,2,0:T(8,128)(2,1)} %all-gather.5.cloned.1.call-done) | non-fusion elementwise | flops 7077888 | bytes 42467328 | tf_op jit(solution)/shard_map/convert_element_type | solution.py:17
  191.4 7.6 %fusion.1 = bf16[8,384,2304]{1,2,0:T(8,128)(2,1)} fusion(f32[2304]{0:T(1024)S(1)} %copy-done.4, f32[8,384]{1,0:T(8,128)S(1)} %add_rsqrt_fusion, f32[8,384,2304]{1,2,0:T(8,128)S(1)} %bitcast.75), kind=kLoop, calls=%fused_computation.5 | loop fusion | flops 21233664 | bytes 42488832 | tf_op jit(solution)/shard_map/convert_element_type | solution.py:19
  199.0 14.1 %fusion.17 = f32[8,384,576]{1,2,0:T(8,128)} fusion(bf16[8,384,2304]{1,2,0:T(8,128)(2,1)} %fusion.1, bf16[2304,1152]{1,0:T(8,128)(2,1)S(1)} %bitcast.81, s32[]{:T(128)S(6)} %select_n.74), kind=kOutput, calls=%fused_computation.39 | convolution fusion | flops 8153726976 | bytes 24182788 | tf_op jit(solution)/shard_map/dot_general | solution.py:223
  213.0 8.4 %copy.113 = f32[8,384,576]{2,1,0:T(8,128)} copy(f32[8,384,576]{1,2,0:T(8,128)} %fusion.17) | data formatting | bytes 14155776 | tf_op jit(solution)/shard_map/dot_general | solution.py:223
  221.4 4.2 dynamic-slice_bitcast_fusion.1
  225.6 58.1 %all-gather.9.cloned.1.call-done = bf16[12288,576]{0,1:T(8,128)(2,1)} async-done(((bf16[384,576]{0,1:T(8,128)(2,1)}), bf16[12288,576]{0,1:T(8,128)(2,1)}) %all-gather.9.cloned.1.call-update) | async-done | bytes 14155792 | tf_op jit(solution)/shard_map/all_gather | solution.py:214
  283.7 22.2 %reshape.57 = bf16[8,4,384,576]{2,1,0,3:T(4,128)(2,1)} reshape(bf16[12288,576]{0,1:T(8,128)(2,1)} %all-gather.9.cloned.1.call-done) | data formatting | bytes 28311552 | tf_op jit(solution)/shard_map/reshape | solution.py:221
  306.0 8.8 %copy.98 = bf16[8,4,384,576]{2,3,1,0:T(8,128)(2,1)S(1)} copy(bf16[8,4,384,576]{2,1,0,3:T(4,128)(2,1)} %reshape.57) | data formatting | bytes 28311552 | tf_op jit(solution)/shard_map/reshape | solution.py:221
  314.8 2.2 dynamic-slice_bitcast_fusion
  317.0 14.0 %fusion.54 = (f32[8,384,576]{1,2,0:T(8,128)}, f32[8,384,576]{1,2,0:T(8,128)}) fusion(f32[8,384,576]{1,2,0:T(8,128)} %fusion.17, bf16[8,384,2304]{1,2,0:T(8,128)(2,1)S(1)} %bitcast.77, bf16[1152,2304]{1,0:T(8,128)(2,1)} %param.13, s32[]{:T(128)S(6)} %select_n.74), kind=kOutput, calls=%fused_computation.89 | convolution fusion | flops 8155496448 | bytes 38043652 | tf_op jit(solution)/shard_map/dot_general | solution.py:226
  331.0 8.4 %copy.108 = f32[8,384,576]{2,1,0:T(8,128)} copy(f32[8,384,576]{1,2,0:T(8,128)} %get-tuple-element.25) | data formatting | bytes 14155776 | tf_op jit(solution)/shard_map/mul | solution.py:229
  339.4 8.5 %copy.112 = f32[8,384,576]{2,1,0:T(8,128)} copy(f32[8,384,576]{1,2,0:T(8,128)} %get-tuple-element.26) | data formatting | bytes 14155776 | tf_op jit(solution)/shard_map/dot_general | solution.py:226
  347.9 5.7 %pad_maximum_fusion.1.left_ref = bf16[2,8,576,384]{3,2,1,0:T(8,128)(2,1)} fusion(bf16[1,8,576,384]{3,2,1,0:T(8,128)(2,1)} %dynamic-slice_bitcast_fusion, bf16[1,8,576,384]{3,2,1,0:T(8,128)(2,1)S(1)} %copy-done.1), kind=kLoop, calls=%fused_computation.20 | loop fusion | flops 3538944 | bytes 14155776 | tf_op jit(solution)/shard_map/stack | solution.py:232
  353.5 27.5 %fusion.11 = (bf16[1,8,384,576]{3,2,1,0:T(8,128)(2,1)}, bf16[1,8,384,576]{3,2,1,0:T(8,128)(2,1)}, bf16[1,8,384,576]{3,2,1,0:T(8,128)(2,1)}) fusion(f32[8,384,576]{2,1,0:T(8,128)} %copy.108, f32[8,384,576]{2,1,0:T(8,128)} %copy.113, f32[8,384,576]{2,1,0:T(8,128)} %copy.112, bf16[8,384,2304]{1,2,0:T(8,128)(2,1)} %fusion.1, bf16[2304,1152]{1,0:T(8,128)(2,1)} %param.11, ...), kind=kOutput, calls=%fused_computation.30 | convolution fusion | flops 8197963776 | bytes 51314692 | tf_op jit(solution)/shard_map/dot_general | solution.py:222
  381.0 10.4 %pad_maximum_fusion.right_ref = bf16[3,8,384,576]{3,2,1,0:T(8,128)(2,1)} fusion(bf16[1,8,384,576]{3,2,1,0:T(8,128)(2,1)} %get-tuple-element.18, bf16[1,8,384,576]{3,2,1,0:T(8,128)(2,1)} %get-tuple-element.19, bf16[1,8,384,576]{3,2,1,0:T(8,128)(2,1)} %get-tuple-element.17), kind=kLoop, calls=%fused_computation.7 | loop fusion | flops 10616832 | bytes 21233664 | tf_op jit(solution)/shard_map/stack | solution.py:238
  391.4 36.8 %deltas_and_gram.1 = (bf16[3,8,576,576]{3,2,1,0:T(8,128)(2,1)}, f32[36,128]{1,0:T(8,128)S(1)}) custom-call(bf16[2,8,576,384]{3,2,1,0:T(8,128)(2,1)} %pad_maximum_fusion.1.left_ref, bf16[3,8,384,576]{3,2,1,0:T(8,128)(2,1)} %pad_maximum_fusion.right_ref), custom_call_target="tpu_custom_call" | custom-call | flops 6115295232 | bytes 41943040 | tf_op jit(solution)/shard_map/deltas_and_gram/pallas_call | solution.py:155
  428.1 0.1 reduce_sum.74
  428.3 0.8 gather_fusion
  429.0 0.1 reshape.65
  429.1 38.6 %psum.7 = f32[8,8]{1,0:T(8,128)S(1)} all-reduce(f32[8,8]{1,0:T(8,128)S(1)} %reshape.65), channel_id=1, replica_groups=mesh['client'=8,'param'=4] {'client','param'}, use_global_device_ids=true, to_apply=%region_5.6 | all-reduce | flops 64 | bytes 512 | tf_op jit(solution)/shard_map/psum | solution.py:239
  467.8 0.6 gather_fusion.1
  468.4 0.1 subtract_select_fusion
  468.5 0.1 copy.114
  468.5 0.7 sort.15
  469.2 0.6 fusion.44
  470.5 0.6 fusion.53
  471.1 1.2 broadcast_multiply_fusion
  472.2 12.7 %multiply_reduce_fusion = f32[3,576,576]{2,1,0:T(8,128)S(1)} fusion(bf16[3,8,576,576]{3,2,1,0:T(8,128)(2,1)} %get-tuple-element.10, f32[8]{0:T(128)S(1)} %get-tuple-element.14), kind=kLoop, calls=%fused_computation.2 | loop fusion | flops 22892544 | bytes 19906592 | tf_op jit(solution)/shard_map/reduce_sum | solution.py:241
  485.0 2.0 copy-done
  487.0 1.5 dynamic-slice_bitcast_fusion.2
  488.5 4.5 collective-permute-done
  493.0 1.9 bitcast_select_fusion
  494.9 2.6 fusion.36
  (27 shorter events, 0.1 us)
Async XLA Ops:
  8.0 38.0 %all-gather.7.cloned.1.call-start = ((), (), s32[]{:S(2)}) async-start(), calls=%async_computation.2 | async-start | bytes 2211840 | tf_op jit(solution)/shard_map/all_gather | solution.py:203
  8.7 94.2 %reduce-scatter.2.cloned.1.call-start = ((), (), s32[]{:S(2)}) async-start(), calls=%async_computation.3 | async-start | bytes 2211840 | tf_op jit(solution)/shard_map/reduce_scatter | solution.py:210
  47.9 7.1 %copy-start.2 = (bf16[1,384,2304]{1,2,0:T(8,128)(2,1)S(1)}, bf16[1,384,2304]{1,2,0:T(8,128)(2,1)}, u32[]{:S(2)}) copy-start(bf16[1,384,2304]{1,2,0:T(8,128)(2,1)} %all-gather.7.cloned.1.call-done) | copy-start | bytes 5308420
  48.0 7.0 %copy-start.4 = (f32[2304]{0:T(1024)S(1)}, f32[2304]{0:T(1024)}, u32[]{:S(2)}) copy-start(f32[2304]{0:T(1024)} %param.10) | copy-start | bytes 27652
  55.0 47.9 %copy-start.3 = (bf16[1,384,576]{1,2,0:T(8,128)(2,1)S(1)}, bf16[1,384,576]{1,2,0:T(8,128)(2,1)}, u32[]{:S(2)}) copy-start(bf16[1,384,576]{1,2,0:T(8,128)(2,1)} %param.9) | copy-start | bytes 1327108
  55.0 49.9 %copy-start.5 = (s32[64]{0:T(128)S(1)}, s32[64]{0:T(128)}, u32[]{:S(2)}) copy-start(s32[64]{0:T(128)} %constant.129) | copy-start | bytes 772
  67.1 108.2 %all-gather.5.cloned.1.call-start = ((), (), s32[]{:S(2)}) async-start(), calls=%async_computation.1 | async-start | bytes 14598144 | tf_op jit(solution)/shard_map/all_gather | solution.py:204
  67.7 216.1 %all-gather.9.cloned.1.call-start = ((), (), s32[]{:S(2)}) async-start(), calls=%async_computation.4 | async-start | bytes 14598144 | tf_op jit(solution)/shard_map/all_gather | solution.py:214
  183.2 15.8 %slice-start = ((s8[5308416]{0:T(1024)(128)(4,1)}), s8[4194304]{0:T(1024)(128)(4,1)S(1)}, s32[]{:S(2)}) async-start(s8[5308416]{0:T(1024)(128)(4,1)} %bitcast.80), calls=%async_computation.5 | async-start | bytes 8388608
  191.4 7.6 %slice-start.1 = ((s8[5308416]{0:T(1024)(128)(4,1)}), s8[1114112]{0:T(1024)(128)(4,1)S(1)}, s32[]{:S(2)}) async-start(s8[5308416]{0:T(1024)(128)(4,1)} %bitcast.80), calls=%async_computation.6 | async-start | bytes 2228224
  339.4 8.5 %copy-start.1 = (bf16[1,8,576,384]{3,2,1,0:T(8,128)(2,1)S(1)}, bf16[1,8,576,384]{3,2,1,0:T(8,128)(2,1)}, u32[]{:S(2)}) copy-start(bf16[1,8,576,384]{3,2,1,0:T(8,128)(2,1)} %dynamic-slice_bitcast_fusion.1) | copy-start | bytes 10616836
  391.4 77.9 %copy-start.6 = (s32[8]{0:T(128)S(1)}, s32[8]{0:T(128)}, u32[]{:S(2)}) copy-start(s32[8]{0:T(128)} %param.14) | copy-start | bytes 100
  485.0 2.0 copy-start
  488.5 4.5 collective-permute-start
Sparse Core Ops, SparseCore 0:
  10.7 35.2 all-gather.6
  67.2 35.6 reduce-scatter.1
Sparse Core Ops, SparseCore 1:
  70.5 104.8 all-gather.4
  178.5 105.1 all-gather.8

commit v2 on v0

--- a/solution.py
+++ b/solution.py
@@ -1,8 +1,11 @@
+import functools
 import math
 
 import jax
 import jax.numpy as jnp
 from jax import lax
+from jax.experimental import pallas as pl
+from jax.experimental.pallas import tpu as pltpu
 from jax.sharding import PartitionSpec as P
 
 
@@ -86,6 +89,277 @@
     update_down = weighted_sum(weights, owned_down)
     return (update_gate, update_up, update_down, client_count * weights)
 
+PAIR = 2
+
+
+def gelu_parts(values):
+    scale = math.sqrt(2.0 / math.pi)
+    squared = values * values
+    bent = jnp.tanh(scale * values * (1.0 + 0.044715 * squared))
+    lifted = 0.5 * (1.0 + bent)
+    slope = 0.5 * values * (1.0 - bent * bent) * scale * (1.0 + 3.0 * 0.044715 * squared)
+    return values * lifted, lifted + slope
+
+
+def forward_kernel(
+    rows_ref, gain_ref, gate_ref, up_ref, slope_ref, active_ref, hidden_ref, block_ref, normed
+):
+    params, _, width = rows_ref.shape
+    chip = lax.axis_index("client") // PAIR
+    total = 0.0
+    for at in range(params):
+        wide = rows_ref[at].astype(jnp.float32)
+        total += jnp.sum(wide * wide, axis=1, keepdims=True)
+    inverse = lax.rsqrt(total * (1.0 / (params * width)) + 1e-06)
+    for at in range(params):
+        wide = rows_ref[at].astype(jnp.float32)
+        normed[:, at * width : (at + 1) * width] = (wide * inverse * gain_ref[at]).astype(jnp.bfloat16)
+    block_ref[...] = (rows_ref[chip].astype(jnp.float32) * inverse * gain_ref[chip]).astype(jnp.bfloat16)
+    gate = jnp.dot(normed[...], gate_ref[...], preferred_element_type=jnp.float32)
+    up = jnp.dot(normed[...], up_ref[...], preferred_element_type=jnp.float32)
+    active, slope = gelu_parts(gate)
+    slope_ref[...] = slope * up
+    active_ref[...] = active
+    hidden_ref[...] = (active * up).astype(jnp.bfloat16)
+
+
+def forward_all(every_input, norm_gain, gate_half, up_half):
+    clients, params, tokens, width = every_input.shape
+    depth, half = gate_half.shape
+    client_block = lambda shape: pl.BlockSpec((None,) + shape, lambda at: (at,) + (0,) * len(shape))
+    whole = lambda shape: pl.BlockSpec(shape, lambda at: (0,) * len(shape))
+    return pl.pallas_call(
+        forward_kernel,
+        grid=(clients,),
+        in_specs=[
+            client_block((params, tokens, width)),
+            whole((params, 1, width)),
+            whole((depth, half)),
+            whole((depth, half)),
+        ],
+        out_specs=[client_block((tokens, half))] * 3 + [client_block((tokens, width))],
+        out_shape=[
+            jax.ShapeDtypeStruct((clients, tokens, half), jnp.float32),
+            jax.ShapeDtypeStruct((clients, tokens, half), jnp.float32),
+            jax.ShapeDtypeStruct((clients, tokens, half), jnp.bfloat16),
+            jax.ShapeDtypeStruct((clients, tokens, width), jnp.bfloat16),
+        ],
+        scratch_shapes=[pltpu.VMEM((tokens, depth), jnp.bfloat16)],
+        compiler_params=pltpu.CompilerParams(vmem_limit_bytes=56 * 2**20),
+        cost_estimate=pl.CostEstimate(
+            flops=4 * clients * tokens * depth * half, bytes_accessed=40 * 2**20, transcendentals=0
+        ),
+        name="forward_all",
+    )(every_input, norm_gain.reshape(params, 1, width), gate_half, up_half)
+
+
+def backward_kernel(
+    rows_ref, slope_ref, active_ref, hidden_ref, block_ref, down_ref, delta_ref, gram_ref,
+    residual, held, totals,
+):
+    params, _, width = rows_ref.shape
+    _, clients, rows, columns = held.shape
+    step_at = pl.program_id(0)
+    chip = lax.axis_index("client") // PAIR
+    for at in range(params):
+        residual[:, at * width : (at + 1) * width] = rows_ref[at]
+    back = lax.dot_general(
+        residual[...], down_ref[...], (((1,), (1,)), ((), ())), preferred_element_type=jnp.float32
+    )
+    back_gate = (back * slope_ref[...]).astype(jnp.bfloat16)
+    back_up = (back * active_ref[...]).astype(jnp.bfloat16)
+    for kind, (left, right) in enumerate(
+        ((block_ref[...], back_gate), (block_ref[...], back_up), (rows_ref[chip], hidden_ref[...]))
+    ):
+        delta = (-token_contract(left, right)).astype(jnp.bfloat16)
+        delta_ref[kind] = delta
+        held[kind, step_at] = delta
+
+    @pl.when(step_at == clients - 1)
+    def _():
+        totals[...] = jnp.zeros_like(totals)
+        pairs = [(i, j) for i in range(clients) for j in range(i, clients)]
+        starts = [(at, min(128, columns - at)) for at in range(0, columns, 128)]
+
+        def add_up(kind, begin, wide, repeat):
+            def step(index, sums):
+                row = pl.multiple_of(index * 16, 16)
+                for at in range(begin, begin + wide * repeat, wide):
+                    tiles = [
+                        held[kind, client, pl.ds(row, 16), at : at + wide].astype(jnp.float32)
+                        for client in range(clients)
+                    ]
+                    found = []
+                    for (i, j), total in zip(pairs, sums):
+                        product = tiles[i] * tiles[j]
+                        found.append(total + (product[:8] + product[8:]))
+                    sums = tuple(found)
+                return sums
+
+            zeros = tuple(jnp.zeros((8, wide), jnp.float32) for _ in pairs)
+            sums = lax.fori_loop(0, rows // 16, step, zeros)
+            for at, total in enumerate(sums):
+                totals[at, :, :wide] += total
+
+        lanes = columns // 128 * 128
+        for kind in range(3):
+            add_up(kind, 0, 128, lanes // 128)
+            if columns - lanes:
+                add_up(kind, lanes, columns - lanes, 1)
+        gram_ref[...] = jnp.zeros_like(gram_ref)
+        gram_ref[: len(pairs), :] = jnp.sum(totals[...], axis=1)
+
+
+def backward_all(every_residual, slope, active, hidden, block, down_half):
+    clients, params, tokens, width = every_residual.shape
+    half, depth = down_half.shape
+    pair_count = clients * (clients + 1) // 2
+    padded = -(-pair_count // 8) * 8
+    client_block = lambda shape: pl.BlockSpec((None,) + shape, lambda at: (at,) + (0,) * len(shape))
+    return pl.pallas_call(
+        backward_kernel,
+        grid=(clients,),
+        in_specs=[client_block((params, tokens, width))]
+        + [client_block((tokens, half))] * 3
+        + [client_block((tokens, width)), pl.BlockSpec((half, depth), lambda at: (0, 0))],
+        out_specs=[
+            pl.BlockSpec((3, None, width, half), lambda at: (0, at, 0, 0)),
+            pl.BlockSpec((padded, 128), lambda at: (0, 0)),
+        ],
+        out_shape=[
+            jax.ShapeDtypeStruct((3, clients, width, half), jnp.bfloat16),
+            jax.ShapeDtypeStruct((padded, 128), jnp.float32),
+        ],
+        scratch_shapes=[
+            pltpu.VMEM((tokens, depth), jnp.bfloat16),
+            pltpu.VMEM((3, clients, width, half), jnp.bfloat16),
+            pltpu.VMEM((pair_count, 8, 128), jnp.float32),
+        ],
+        compiler_params=pltpu.CompilerParams(vmem_limit_bytes=60 * 2**20),
+        cost_estimate=pl.CostEstimate(
+            flops=2 * clients * tokens * (depth + 3 * width) * half,
+            bytes_accessed=50 * 2**20,
+            transcendentals=0,
+        ),
+        name="backward_all",
+    )(every_residual, slope, active, hidden, block, down_half)
+
+
+def sum_kernel(part_ref, total_ref, params_held, clients_held, summed, sends, receives):
+    clients, params = clients_held.shape[0], params_held.shape[0]
+    client, param = lax.axis_index("client"), lax.axis_index("param")
+    barrier = pltpu.get_barrier_semaphore()
+    for step in range(1, params):
+        pl.semaphore_signal(
+            barrier, inc=1, device_id=(client, lax.rem(param + step, params)),
+            device_id_type=pl.DeviceIdType.MESH,
+        )
+    for step in range(1, clients):
+        pl.semaphore_signal(
+            barrier, inc=1, device_id=(lax.rem(client + step, clients), param),
+            device_id_type=pl.DeviceIdType.MESH,
+        )
+    pl.semaphore_wait(barrier, params + clients - 2)
+
+    def exchange(source, held, me, count, target, first):
+        held[me] = source[...]
+        copies = []
+        for step in range(1, count):
+            copy = pltpu.make_async_remote_copy(
+                src_ref=source,
+                dst_ref=held.at[me],
+                send_sem=sends.at[first + step],
+                recv_sem=receives.at[first + step],
+                device_id=target(lax.rem(me + step, count)),
+                device_id_type=pl.DeviceIdType.MESH,
+            )
+            copy.start()
+            copies.append(copy)
+        for copy in copies:
+            copy.wait()
+        total = held[0]
+        for at in range(1, count):
+            total = total + held[at]
+        return total
+
+    summed[...] = exchange(part_ref, params_held, param, params, lambda to: (client, to), 0)
+    total_ref[...] = exchange(summed, clients_held, client, clients, lambda to: (to, param), params)
+
+
+def sum_everywhere(part):
+    clients, params = lax.axis_size("client"), lax.axis_size("param")
+    return pl.pallas_call(
+        sum_kernel,
+        in_specs=[pl.BlockSpec(memory_space=pltpu.VMEM)],
+        out_specs=pl.BlockSpec(memory_space=pltpu.VMEM),
+        out_shape=jax.ShapeDtypeStruct(part.shape, part.dtype),
+        scratch_shapes=[
+            pltpu.VMEM((params,) + part.shape, part.dtype),
+            pltpu.VMEM((clients,) + part.shape, part.dtype),
+            pltpu.VMEM(part.shape, part.dtype),
+            pltpu.SemaphoreType.DMA((params + clients,)),
+            pltpu.SemaphoreType.DMA((params + clients,)),
+        ],
+        compiler_params=pltpu.CompilerParams(collective_id=0, has_side_effects=True),
+        name="sum_everywhere",
+    )(part)
+
+
+def place_count(clients, i, j):
+    return i * clients - i * (i - 1) // 2 + (j - i)
+
+
+def on_device_shared(inputs, targets, norm_gain, gate_weight, up_weight, down_weight, neighbours):
+    token_count = inputs.shape[1]
+    clients = lax.axis_size("client")
+    params = lax.axis_size("param")
+    client = lax.axis_index("client")
+    width = inputs.shape[2]
+    depth = width * params
+    core = client % PAIR
+    half = gate_weight.shape[1] // PAIR
+    chip_rows = depth // clients * PAIR
+    factor = 1.0 / math.sqrt(token_count)
+
+    own = lax.all_gather(inputs, "param", axis=2, tiled=True)[0]
+    every_input = lax.all_gather(inputs[0], ("client", "param"), axis=0)
+    normed_own = rms_normed(own, norm_gain)
+    gate_value = jnp.dot(normed_own, gate_weight, preferred_element_type=jnp.float32)
+    up_value = jnp.dot(normed_own, up_weight, preferred_element_type=jnp.float32)
+    hidden = (gelu_tanh(gate_value) * up_value).astype(jnp.bfloat16)
+    partial_out = jnp.dot(hidden, down_weight, preferred_element_type=jnp.float32)
+    out_share = lax.psum_scatter(
+        partial_out.astype(jnp.bfloat16), "param", scatter_dimension=1, tiled=True
+    ).astype(jnp.float32)
+    local_residual = ((out_share - targets[0].astype(jnp.float32)) * factor).astype(jnp.bfloat16)
+    every_residual = lax.all_gather(local_residual, ("client", "param"), axis=0)
+
+    gate_half = lax.dynamic_slice_in_dim(gate_weight, core * half, half, 1)
+    up_half = lax.dynamic_slice_in_dim(up_weight, core * half, half, 1)
+    down_half = lax.dynamic_slice_in_dim(down_weight, core * half, half, 0)
+    shape = (clients, params, token_count, width)
+    slope, active, hidden, block = forward_all(
+        every_input.reshape(shape), norm_gain, gate_half, up_half
+    )
+    deltas, partial_gram = backward_all(
+        every_residual.reshape(shape), slope, active, hidden, block, down_half
+    )
+    upper = jnp.sum(sum_everywhere(partial_gram), axis=1)
+    order = [
+        [place_count(clients, min(i, j), max(i, j)) for j in range(clients)] for i in range(clients)
+    ]
+    gram = upper[jnp.asarray(order)]
+    weights = krum_weights(gram, neighbours)
+    updates = jnp.sum(weights[None, :, None, None] * deltas.astype(jnp.float32), axis=1)
+    updates = updates.reshape(3, PAIR, chip_rows // PAIR, half)
+    kept = lax.dynamic_index_in_dim(updates, core, 1, keepdims=False)
+    sent = lax.dynamic_index_in_dim(updates, 1 - core, 1, keepdims=False)
+    arrived = lax.ppermute(sent, "client", [(i, i ^ 1) for i in range(clients)])
+    first = jnp.where(core == 0, kept, arrived)
+    second = jnp.where(core == 0, arrived, kept)
+    whole = jnp.concatenate([first, second], axis=2)
+    return (whole[0], whole[1], whole[2], clients * weights)
+
 
 def solution(mesh):
     in_specs = (
@@ -98,6 +372,8 @@
         P(),
     )
     out_specs = (P("client", "param"), P("client", "param"), P("client", "param"), P())
+    shared = mesh.shape["client"] <= 8 and mesh.shape["client"] == PAIR * mesh.shape["param"]
+    body = on_device_shared if shared else on_device
     return jax.shard_map(
-        on_device, mesh=mesh, in_specs=in_specs, out_specs=out_specs, check_vma=False
-    )
+        body, mesh=mesh, in_specs=in_specs, out_specs=out_specs, check_vma=False
+    )

time: 669 us -> 400 us (0.60); the launches traced: 661 us -> 399 us
  local copies, waits for them, and re-layouts: 180 us -> 57.1 us
  other arithmetic: 118 us -> 25.1 us
  Pallas kernels: 0 us -> 89.4 us
  waiting for transfers between devices: 256 us -> 192 us
  blocking collectives: 36.9 us -> 0 us
  matrix products: 40.5 us -> 19.1 us
  starting transfers between devices: 14.9 us -> 0.38 us
    all_to_all x3 -> x0, waiting for transfers between devices: 153 us -> none  [the longest x1 79.6 us: on_device(): lax.all_to_all(down_delta[None], 'client', split_axis=1, concat_axis=0, t...]
    broadcast_in_dim x3 -> x0, local copies, waits for them, and re-layouts: 106 us -> none  [the longest x1 35.3 us: on_device(): gate_delta[None]]
    unnamed x7 -> x1, other arithmetic: 101 us -> 0.01 us
    pallas_call x0 -> x3, Pallas kernels: none -> 89.4 us  [the longest x1 44.8 us: backward_all(): pl.pallas_call(backward_kernel, grid=(clients,), in_specs=[client_block((...]
    all_gather x2 -> x3, waiting for transfers between devices: 70.3 us -> 151 us  [the longest x1 57.5 us: on_device_shared(): every_input = lax.all_gather(inputs[0], ('client', 'param'), axis=0)]
    unnamed x46 -> x16, local copies, waits for them, and re-layouts: 73.1 us -> 2.04 us
    all_gather x0 -> x2, local copies, waits for them, and re-layouts: none -> 39.2 us  [the longest x1 20.4 us: on_device_shared(): every_residual = lax.all_gather(local_residual, ('client', 'param'), axis=0)]
    psum x1 -> x0, blocking collectives: 36.9 us -> none  [on_device(): gram = lax.psum(partial_gram, ('client', 'param'))]
  transfers between devices with their start and end apart: 6 -> 5, of which waited for: 6 -> 5; matrix products, arithmetic and copies ran while one was open for 30% -> 8% of each run, Pallas kernels for 0% -> 8%
where the time goes in v2:
time: 400 us; the launch traced here: 399 us
  waiting for transfers between devices  192 us (48%)
  Pallas kernels  89.4 us (22%)
  local copies, waits for them, and re-layouts  57.1 us (14%)
  other arithmetic  25.1 us (6%)
  matrix products  19.1 us (5%)
  between operations  16.2 us (4%)
    all_gather x1, waiting for transfers between devices, on_device_shared(): every_input = lax.all_gather(inputs[0], ('client', 'param'), axis=0)  57.5 us
    all_gather x1, waiting for transfers between devices, on_device_shared(): every_residual = lax.all_gather(local_residual, ('client', 'param'), axis=0)  56.2 us
    pallas_call x1, Pallas kernels, backward_all(): pl.pallas_call(backward_kernel, grid=(clients,), in_specs=[client_block((...  44.8 us
    all_gather x1, waiting for transfers between devices, on_device_shared(): own = lax.all_gather(inputs, 'param', axis=2, tiled=True)[0]  37.2 us
    reduce_scatter x1, waiting for transfers between devices, on_device_shared(): lax.psum_scatter(partial_out.astype(jnp.bfloat16), 'param', scatter_dimen...  35 us
    pallas_call x1, Pallas kernels, forward_all(): pl.pallas_call(forward_kernel, grid=(clients,), in_specs=[client_block((p...  33.4 us
    all_gather x1, local copies, waits for them, and re-layouts, on_device_shared(): every_residual = lax.all_gather(local_residual, ('client', 'param'), axis=0)  20.4 us
    all_gather x1, local copies, waits for them, and re-layouts, on_device_shared(): every_input = lax.all_gather(inputs[0], ('client', 'param'), axis=0)  18.8 us
  transfers between devices with their start and end apart: 5, of which 5 were waited for; matrix products, arithmetic and copies ran while one was open for 8% of the time, Pallas kernels for 8%

profile of v2, /device:TPU:0, one launch (start us, length us, event | category | flops | bytes accessed | tf_op | source)
XLA Modules:
  0.0 399.0 jit_solution(358961989321150583)
XLA Ops:
  8.0 0.0 all-gather.5.cloned.1.call-start
  8.0 0.7 all-gather.5.cloned.1.call-update
  8.7 0.0 reduce-scatter.2.cloned.1.call-start
  8.8 37.2 %all-gather.5.cloned.1.call-done = bf16[1,384,2304]{1,2,0:T(8,128)(2,1)} async-done(((bf16[1,384,576]{1,2,0:T(8,128)(2,1)}), bf16[1,384,2304]{1,2,0:T(8,128)(2,1)}) %all-gather.5.cloned.1.call-update) | async-done | bytes 1769488 | tf_op jit(solution)/shard_map/all_gather | solution.py:324
  46.0 1.9 fusion
  48.0 0.0 copy-start.3
  48.0 7.0 %fusion.20 = f32[384,1152]{1,0:T(8,128)} fusion(bf16[2304,1152]{1,0:T(8,128)(2,1)} %param.11, bf16[1,384,2304]{1,2,0:T(8,128)(2,1)} %all-gather.5.cloned.1.call-done, f32[2304]{0:T(1024)} %param.10, f32[384]{0:T(512)S(1)} %add_rsqrt_fusion), kind=kOutput, calls=%fused_computation.35 | convolution fusion | flops 2041970688 | bytes 8858112 | tf_op jit(solution)/shard_map/dot_general | solution.py:327
  55.0 0.0 copy-done.1
  55.0 0.0 copy-done.3
  55.0 12.1 %convolution_convert_fusion = bf16[384,2304]{0,1:T(8,128)(2,1)} fusion(bf16[1152,2304]{1,0:T(8,128)(2,1)} %param.13, bf16[2304,1152]{1,0:T(8,128)(2,1)} %param.12, f32[384,1152]{1,0:T(8,128)} %fusion.20, bf16[1,384,2304]{1,2,0:T(8,128)(2,1)S(1)} %copy-done.1, f32[2304]{0:T(1024)S(1)} %copy-done.3, f32[384]{0:T(512)S(1)} %add_rsqrt_fusion), kind=kOutput, calls=%fused_computation.9 | convolution fusion | flops 4085710848 | bytes 15936000 | tf_op jit(solution)/shard_map/dot_general | solution.py:330
  67.1 0.0 reduce-scatter.2.cloned.1.call-update
  67.1 0.0 all-gather.7.cloned.1.call-start
  67.1 0.5 all-gather.7.cloned.1.call-update
  67.7 0.2 all-gather.9.cloned.1.call-start
  67.9 35.0 %reduce-scatter.2.cloned.1.call-done = bf16[384,576]{0,1:T(8,128)(2,1)} async-done(((bf16[384,2304]{0,1:T(8,128)(2,1)}), bf16[384,576]{0,1:T(8,128)(2,1)}) %reduce-scatter.2.cloned.1.call-update) | async-done | bytes 442384 | tf_op jit(solution)/shard_map/reduce_scatter | solution.py:331
  102.9 0.0 copy-done.2
  102.9 2.0 fusion.17
  104.9 0.0 all-gather.9.cloned.1.call-update
  104.9 0.7 reshape.44.gain_ref
  105.7 0.0 slice-start.1
  105.7 3.6 constant_dynamic-slice_fusion.down_ref
  109.3 5.2 %constant_dynamic-slice_fusion.1.up_ref = bf16[2304,576]{1,0:T(8,128)(2,1)} fusion(bf16[2304,1152]{1,0:T(8,128)(2,1)} %param.12, s32[]{:T(128)S(6)} %select_n.64), kind=kLoop, calls=%fused_computation.45 | loop fusion | bytes 5308420 | tf_op jit(solution)/shard_map/dynamic_slice | solution.py:338
  114.5 3.2 constant_dynamic-slice_fusion.2.gate_ref
  117.7 57.5 %all-gather.7.cloned.1.call-done = bf16[32,384,576]{1,2,0:T(8,128)(2,1)} async-done(((bf16[1,384,576]{1,2,0:T(8,128)(2,1)}), bf16[32,384,576]{1,2,0:T(8,128)(2,1)}) %all-gather.7.cloned.1.call-update) | async-done | bytes 14155792 | tf_op jit(solution)/shard_map/all_gather | solution.py:325
  175.3 18.8 %copy.18 = bf16[32,384,576]{2,1,0:T(8,128)(2,1)} copy(bf16[32,384,576]{1,2,0:T(8,128)(2,1)} %all-gather.7.cloned.1.call-done) | data formatting | bytes 28311552 | tf_op jit(solution)/shard_map/all_gather | solution.py:325
  194.1 33.4 %forward_all.1 = (f32[8,384,576]{2,1,0:T(8,128)}, f32[8,384,576]{2,1,0:T(8,128)}, bf16[8,384,576]{2,1,0:T(8,128)(2,1)}, bf16[8,384,576]{2,1,0:T(8,128)(2,1)}) custom-call(bf16[8,4,384,576]{3,2,1,0:T(8,128)(2,1)} %bitcast.32, f32[4,1,576]{2,1,0:T(1,128)} %reshape.44.gain_ref, bf16[2304,576]{1,0:T(8,128)(2,1)} %constant_dynamic-slice_fusion.2.gate_ref, ...), custom_call_target="tpu_custom_call" | custom-call | flops 16307453952 | bytes 41943040 | tf_op jit(solution)/shard_map/forward_all/pallas_call | solution.py:131
  227.5 56.2 %all-gather.9.cloned.1.call-done = bf16[12288,576]{0,1:T(8,128)(2,1)} async-done(((bf16[384,576]{0,1:T(8,128)(2,1)}), bf16[12288,576]{0,1:T(8,128)(2,1)}) %all-gather.9.cloned.1.call-update) | async-done | bytes 14155792 | tf_op jit(solution)/shard_map/all_gather | solution.py:335
  283.7 20.4 %copy.17 = bf16[12288,576]{1,0:T(8,128)(2,1)} copy(bf16[12288,576]{0,1:T(8,128)(2,1)} %all-gather.9.cloned.1.call-done) | data formatting | bytes 28311552 | tf_op jit(solution)/shard_map/all_gather | solution.py:335
  304.1 44.8 %backward_all.1 = (bf16[3,8,576,576]{3,2,1,0:T(8,128)(2,1)}, f32[40,128]{1,0:T(8,128)}) custom-call(bf16[8,4,384,576]{3,2,1,0:T(8,128)(2,1)} %bitcast.31, f32[8,384,576]{2,1,0:T(8,128)} %get-tuple-element.12.slope_ref, f32[8,384,576]{2,1,0:T(8,128)} %get-tuple-element.13.active_ref, bf16[8,384,576]{2,1,0:T(8,128)(2,1)} %get-tuple-element.14.hidden_ref, ...), custom_call_target="tpu_custom_call" | custom-call | flops 14269022208 | bytes 52428800 | tf_op jit(solution)/shard_map/backward_all/pallas_call | solution.py:219
  348.8 11.3 %sum_everywhere.1 = f32[40,128]{1,0:T(8,128)} custom-call(f32[40,128]{1,0:T(8,128)} %get-tuple-element.16.part_ref), custom_call_target="tpu_custom_call" | custom-call | tf_op jit(solution)/shard_map/sum_everywhere/pallas_call | solution.py:291
  360.1 0.8 reduce_sum.55
  361.0 0.8 gather_fusion
  361.8 0.1 reshape.49
  361.8 0.1 copy.19
  361.9 0.6 gather_fusion.1
  362.6 0.1 subtract_select_fusion
  362.6 0.7 sort.15
  363.3 0.6 fusion.23
  364.6 0.6 fusion.29
  365.2 1.2 broadcast_multiply_fusion
  366.3 12.7 %multiply_reduce_fusion = f32[3,576,576]{2,1,0:T(8,128)S(1)} fusion(bf16[3,8,576,576]{3,2,1,0:T(8,128)(2,1)} %get-tuple-element.18, f32[8]{0:T(128)S(1)} %get-tuple-element.22), kind=kLoop, calls=%fused_computation.2 | loop fusion | flops 22892544 | bytes 19906592 | tf_op jit(solution)/shard_map/reduce_sum | solution.py:353
  379.1 0.0 copy-start
  379.1 2.0 copy-done
  381.1 1.5 dynamic-slice_bitcast_fusion
  382.6 0.0 collective-permute-start
  382.6 4.5 %collective-permute-done = f32[3,288,576]{2,1,0:T(8,128)S(1)} collective-permute-done((f32[3,288,576]{2,1,0:T(8,128)}, f32[3,288,576]{2,1,0:T(8,128)S(1)}, u32[]{:S(2)}, u32[]{:S(2)}) %collective-permute-start) | collective-permute-done | bytes 1990688 | tf_op jit(solution)/shard_map/ppermute | solution.py:357
  387.1 1.9 bitcast_select_fusion
  389.1 2.6 fusion.15
  (14 shorter events, 0.0 us)
Async XLA Ops:
  8.0 38.0 %all-gather.5.cloned.1.call-start = ((), (), s32[]{:S(2)}) async-start(), calls=%async_computation.1 | async-start | bytes 2211840 | tf_op jit(solution)/shard_map/all_gather | solution.py:324
  8.7 94.2 %reduce-scatter.2.cloned.1.call-start = ((), (), s32[]{:S(2)}) async-start(), calls=%async_computation.2 | async-start | bytes 2211840 | tf_op jit(solution)/shard_map/reduce_scatter | solution.py:331
  47.9 7.0 %copy-start.1 = (bf16[1,384,2304]{1,2,0:T(8,128)(2,1)S(1)}, bf16[1,384,2304]{1,2,0:T(8,128)(2,1)}, u32[]{:S(2)}) copy-start(bf16[1,384,2304]{1,2,0:T(8,128)(2,1)} %all-gather.5.cloned.1.call-done) | copy-start | bytes 5308420
  48.0 7.0 %copy-start.3 = (f32[2304]{0:T(1024)S(1)}, f32[2304]{0:T(1024)}, u32[]{:S(2)}) copy-start(f32[2304]{0:T(1024)} %param.10) | copy-start | bytes 27652
  55.0 47.9 %copy-start.2 = (bf16[1,384,576]{1,2,0:T(8,128)(2,1)S(1)}, bf16[1,384,576]{1,2,0:T(8,128)(2,1)}, u32[]{:S(2)}) copy-start(bf16[1,384,576]{1,2,0:T(8,128)(2,1)} %param.9) | copy-start | bytes 1327108
  67.1 38.6 %copy-start.4 = (s32[64]{0:T(128)S(1)}, s32[64]{0:T(128)}, u32[]{:S(2)}) copy-start(s32[64]{0:T(128)} %constant.105) | copy-start | bytes 772
  67.1 108.2 %all-gather.7.cloned.1.call-start = ((), (), s32[]{:S(2)}) async-start(), calls=%async_computation.3 | async-start | bytes 14598144 | tf_op jit(solution)/shard_map/all_gather | solution.py:325
  67.7 216.0 %all-gather.9.cloned.1.call-start = ((), (), s32[]{:S(2)}) async-start(), calls=%async_computation.4 | async-start | bytes 14598144 | tf_op jit(solution)/shard_map/all_gather | solution.py:335
  102.9 11.6 %slice-start = ((s8[5308416]{0:T(1024)(128)(4,1)}), s8[1114112]{0:T(1024)(128)(4,1)S(1)}, s32[]{:S(2)}) async-start(s8[5308416]{0:T(1024)(128)(4,1)} %bitcast.33), calls=%async_computation.5 | async-start | bytes 2228224
  105.7 8.9 %slice-start.1 = ((s8[5308416]{0:T(1024)(128)(4,1)}), s8[4194304]{0:T(1024)(128)(4,1)S(1)}, s32[]{:S(2)}) async-start(s8[5308416]{0:T(1024)(128)(4,1)} %bitcast.33), calls=%async_computation.6 | async-start | bytes 8388608
  348.8 14.5 %copy-start.5 = (s32[8]{0:T(128)S(1)}, s32[8]{0:T(128)}, u32[]{:S(2)}) copy-start(s32[8]{0:T(128)} %param.14) | copy-start | bytes 100
  379.1 2.0 copy-start
  382.6 4.5 %collective-permute-start = (f32[3,288,576]{2,1,0:T(8,128)}, f32[3,288,576]{2,1,0:T(8,128)S(1)}, u32[]{:S(2)}, u32[]{:S(2)}) collective-permute-start(f32[3,288,576]{2,1,0:T(8,128)} %dynamic-slice_bitcast_fusion), channel_id=1, source_target_pairs={{0,4},{4,0},{8,12},{12,8},{16,20},{20,16},{24,28},{28,24},{1,5},{5... | collective-permute-start | bytes 5971976 | tf_op jit(solution)/shard_map/ppermute | solution.py:357
Sparse Core Ops, SparseCore 0:
  10.7 35.2 all-gather.4
  67.2 35.6 reduce-scatter.1
Sparse Core Ops, SparseCore 1:
  70.5 104.8 all-gather.6
  178.5 105.1 all-gather.8

commit v3 on v2

--- a/solution.py
+++ b/solution.py
@@ -104,17 +104,17 @@
 def forward_kernel(
     rows_ref, gain_ref, gate_ref, up_ref, slope_ref, active_ref, hidden_ref, block_ref, normed
 ):
-    params, _, width = rows_ref.shape
+    params, width = rows_ref.shape[0], rows_ref.shape[2] // 2
     chip = lax.axis_index("client") // PAIR
     total = 0.0
     for at in range(params):
-        wide = rows_ref[at].astype(jnp.float32)
+        wide = unpacked(rows_ref[at]).astype(jnp.float32)
         total += jnp.sum(wide * wide, axis=1, keepdims=True)
     inverse = lax.rsqrt(total * (1.0 / (params * width)) + 1e-06)
     for at in range(params):
-        wide = rows_ref[at].astype(jnp.float32)
+        wide = unpacked(rows_ref[at]).astype(jnp.float32)
         normed[:, at * width : (at + 1) * width] = (wide * inverse * gain_ref[at]).astype(jnp.bfloat16)
-    block_ref[...] = (rows_ref[chip].astype(jnp.float32) * inverse * gain_ref[chip]).astype(jnp.bfloat16)
+    block_ref[...] = (unpacked(rows_ref[chip]).astype(jnp.float32) * inverse * gain_ref[chip]).astype(jnp.bfloat16)
     gate = jnp.dot(normed[...], gate_ref[...], preferred_element_type=jnp.float32)
     up = jnp.dot(normed[...], up_ref[...], preferred_element_type=jnp.float32)
     active, slope = gelu_parts(gate)
@@ -124,7 +124,8 @@
 
 
 def forward_all(every_input, norm_gain, gate_half, up_half):
-    clients, params, tokens, width = every_input.shape
+    clients, params, rows, lanes = every_input.shape
+    tokens, width = 2 * rows, lanes // 2
     depth, half = gate_half.shape
     client_block = lambda shape: pl.BlockSpec((None,) + shape, lambda at: (at,) + (0,) * len(shape))
     whole = lambda shape: pl.BlockSpec(shape, lambda at: (0,) * len(shape))
@@ -132,7 +133,7 @@
         forward_kernel,
         grid=(clients,),
         in_specs=[
-            client_block((params, tokens, width)),
+            client_block((params, rows, lanes)),
             whole((params, 1, width)),
             whole((depth, half)),
             whole((depth, half)),
@@ -157,19 +158,19 @@
     rows_ref, slope_ref, active_ref, hidden_ref, block_ref, down_ref, delta_ref, gram_ref,
     residual, held, totals,
 ):
-    params, _, width = rows_ref.shape
+    params, width = rows_ref.shape[0], rows_ref.shape[2] // 2
     _, clients, rows, columns = held.shape
     step_at = pl.program_id(0)
     chip = lax.axis_index("client") // PAIR
     for at in range(params):
-        residual[:, at * width : (at + 1) * width] = rows_ref[at]
+        residual[:, at * width : (at + 1) * width] = unpacked(rows_ref[at])
     back = lax.dot_general(
         residual[...], down_ref[...], (((1,), (1,)), ((), ())), preferred_element_type=jnp.float32
     )
     back_gate = (back * slope_ref[...]).astype(jnp.bfloat16)
     back_up = (back * active_ref[...]).astype(jnp.bfloat16)
     for kind, (left, right) in enumerate(
-        ((block_ref[...], back_gate), (block_ref[...], back_up), (rows_ref[chip], hidden_ref[...]))
+        ((block_ref[...], back_gate), (block_ref[...], back_up), (unpacked(rows_ref[chip]), hidden_ref[...]))
     ):
         delta = (-token_contract(left, right)).astype(jnp.bfloat16)
         delta_ref[kind] = delta
@@ -211,7 +212,8 @@
 
 
 def backward_all(every_residual, slope, active, hidden, block, down_half):
-    clients, params, tokens, width = every_residual.shape
+    clients, params, packed_rows, lanes = every_residual.shape
+    tokens, width = 2 * packed_rows, lanes // 2
     half, depth = down_half.shape
     pair_count = clients * (clients + 1) // 2
     padded = -(-pair_count // 8) * 8
@@ -219,7 +221,7 @@
     return pl.pallas_call(
         backward_kernel,
         grid=(clients,),
-        in_specs=[client_block((params, tokens, width))]
+        in_specs=[client_block((params, packed_rows, lanes))]
         + [client_block((tokens, half))] * 3
         + [client_block((tokens, width)), pl.BlockSpec((half, depth), lambda at: (0, 0))],
         out_specs=[
@@ -243,6 +245,160 @@
         ),
         name="backward_all",
     )(every_residual, slope, active, hidden, block, down_half)
+
+
+COLUMN, ACROSS, ALONG, FIRST, SECOND, SHARED, DOWN = 0, 1, 2, 3, 4, 5, 10
+
+
+def gather_kernel(block_ref, all_ref, local_sem, sends, receives):
+    clients, params, rows, _ = all_ref.shape
+    chips = clients // PAIR
+    client, param = lax.axis_index("client"), lax.axis_index("param")
+    chip, core = client // PAIR, lax.rem(client, PAIR)
+    across = param + 1 - 2 * lax.rem(param, 2)
+    along = param + 2 - 4 * (param // 2)
+    far = params - 1 - param
+    sibling = (client + 1 - 2 * core, param)
+    to_across, to_along = (client, across), (client, along)
+    above, below = (client + PAIR, param), (client - PAIR, param)
+
+    barrier = pltpu.get_barrier_semaphore()
+
+    def greet(target):
+        pl.semaphore_signal(barrier, inc=1, device_id=target, device_id_type=pl.DeviceIdType.MESH)
+
+    for target in (sibling, to_across, to_along):
+        greet(target)
+    pl.when(chip + 1 < chips)(lambda: greet(above))
+    pl.when(chip > 0)(lambda: greet(below))
+    beside = (chip + chips - 1) // chips + (2 * chips - 2 - chip) // chips
+    pl.semaphore_wait(barrier, 3 + beside)
+
+    def place(origin, owner, kind=COLUMN, of=core):
+        whole = all_ref.at[origin * PAIR + of, owner]
+        if kind == FIRST:
+            return whole.at[pl.ds(0, rows // 2)]
+        if kind == SECOND:
+            return whole.at[pl.ds(rows // 2, rows // 2)]
+        return whole
+
+    def copy(source, landing, origin, send_kind, receive_kind, target):
+        return pltpu.make_async_remote_copy(
+            src_ref=source,
+            dst_ref=landing,
+            send_sem=sends.at[origin, send_kind],
+            recv_sem=receives.at[origin, receive_kind],
+            device_id=target,
+            device_id_type=pl.DeviceIdType.MESH,
+        )
+
+    def arrived(origin, kind, landing):
+        copy(landing, landing, origin, kind, kind, sibling).wait_recv()
+
+    def share(origin, owner, kind, source=None):
+        landing = place(origin, owner, kind)
+        source = landing if source is None else source
+        copy(source, landing, origin, SHARED + kind, SHARED + kind, sibling).start()
+
+    def from_column(origin, steps, upward):
+        landing = place(origin, param)
+        source = block_ref
+        if steps:
+            arrived(origin, COLUMN, landing)
+            source = landing
+        if upward or not steps:
+            pl.when(chip + 1 < chips)(
+                lambda: copy(source, landing, origin, COLUMN, COLUMN, above).start()
+            )
+        if not upward or not steps:
+            pl.when(chip > 0)(lambda: copy(source, landing, origin, DOWN, COLUMN, below).start())
+        copy(source, landing, origin, ACROSS, ACROSS, to_across).start()
+        copy(source, landing, origin, ALONG, ALONG, to_along).start()
+        share(origin, param, COLUMN, source)
+
+    def from_sides(origin):
+        landing = place(origin, across)
+        arrived(origin, ACROSS, landing)
+        part = place(origin, across, FIRST)
+        copy(part, part, origin, FIRST, FIRST, to_along).start()
+        share(origin, across, ACROSS)
+        landing = place(origin, along)
+        arrived(origin, ALONG, landing)
+        part = place(origin, along, SECOND)
+        copy(part, part, origin, SECOND, SECOND, to_across).start()
+        share(origin, along, ALONG)
+
+    def from_corner(origin):
+        for kind in (FIRST, SECOND):
+            arrived(origin, kind, place(origin, far, kind))
+            share(origin, far, kind)
+
+    def finish(origin, steps, upward):
+        owners = {COLUMN: param, ACROSS: across, ALONG: along, FIRST: far, SECOND: far}
+        for kind, owner in owners.items():
+            arrived(origin, SHARED + kind, place(origin, owner, kind, 1 - core))
+            landing = place(origin, owner, kind)
+            copy(landing, landing, origin, SHARED + kind, SHARED + kind, sibling).wait_send()
+        whole, part = place(origin, param), place(origin, across, FIRST)
+
+        def sent(source, kind):
+            copy(source, source, origin, kind, kind, sibling).wait_send()
+
+        sent(whole, ACROSS)
+        sent(whole, ALONG)
+        sent(part, FIRST)
+        sent(part, SECOND)
+        if upward or not steps:
+            pl.when(chip + 1 < chips)(lambda: sent(whole, COLUMN))
+        if not upward or not steps:
+            pl.when(chip > 0)(lambda: sent(whole, DOWN))
+
+    kept = pltpu.make_async_copy(block_ref, all_ref.at[client, param], local_sem)
+    kept.start()
+
+    def visit(steps, stage):
+        if not 0 <= steps < chips:
+            return
+        if steps == 0:
+            stage(chip, 0, True)
+            return
+        pl.when(chip >= steps)(lambda: stage(chip - steps, steps, True))
+        pl.when(chip + steps < chips)(lambda: stage(chip + steps, steps, False))
+
+    for steps in range(chips + 2):
+        visit(steps, from_column)
+        visit(steps - 1, lambda origin, at, upward: from_sides(origin))
+        visit(steps - 2, lambda origin, at, upward: from_corner(origin))
+    for steps in range(chips):
+        visit(steps, finish)
+    kept.wait()
+
+
+def packed(block):
+    rows = block.shape[0] // 2
+    return jnp.concatenate([block[:rows], block[rows:]], axis=1)
+
+
+def unpacked(block):
+    width = block.shape[1] // 2
+    return jnp.concatenate([block[:, :width], block[:, width:]], axis=0)
+
+
+def gather_everything(block):
+    clients, params = lax.axis_size("client"), lax.axis_size("param")
+    return pl.pallas_call(
+        gather_kernel,
+        in_specs=[pl.BlockSpec(memory_space=pl.ANY)],
+        out_specs=pl.BlockSpec(memory_space=pl.ANY),
+        out_shape=jax.ShapeDtypeStruct((clients, params) + block.shape, block.dtype),
+        scratch_shapes=[
+            pltpu.SemaphoreType.DMA,
+            pltpu.SemaphoreType.DMA((clients // PAIR, 11)),
+            pltpu.SemaphoreType.DMA((clients // PAIR, 10)),
+        ],
+        compiler_params=pltpu.CompilerParams(collective_id=1, has_side_effects=True),
+        name="gather_everything",
+    )(block)
 
 
 def sum_kernel(part_ref, total_ref, params_held, clients_held, summed, sends, receives):
@@ -321,8 +477,9 @@
     chip_rows = depth // clients * PAIR
     factor = 1.0 / math.sqrt(token_count)
 
-    own = lax.all_gather(inputs, "param", axis=2, tiled=True)[0]
-    every_input = lax.all_gather(inputs[0], ("client", "param"), axis=0)
+    every_input = gather_everything(packed(inputs[0]))
+    own = lax.dynamic_index_in_dim(every_input, client, 0, keepdims=False)
+    own = jnp.concatenate([unpacked(own[at]) for at in range(params)], axis=1)
     normed_own = rms_normed(own, norm_gain)
     gate_value = jnp.dot(normed_own, gate_weight, preferred_element_type=jnp.float32)
     up_value = jnp.dot(normed_own, up_weight, preferred_element_type=jnp.float32)
@@ -332,17 +489,16 @@
         partial_out.astype(jnp.bfloat16), "param", scatter_dimension=1, tiled=True
     ).astype(jnp.float32)
     local_residual = ((out_share - targets[0].astype(jnp.float32)) * factor).astype(jnp.bfloat16)
-    every_residual = lax.all_gather(local_residual, ("client", "param"), axis=0)
+    every_residual = gather_everything(packed(local_residual))
 
     gate_half = lax.dynamic_slice_in_dim(gate_weight, core * half, half, 1)
     up_half = lax.dynamic_slice_in_dim(up_weight, core * half, half, 1)
     down_half = lax.dynamic_slice_in_dim(down_weight, core * half, half, 0)
-    shape = (clients, params, token_count, width)
     slope, active, hidden, block = forward_all(
-        every_input.reshape(shape), norm_gain, gate_half, up_half
+        every_input, norm_gain, gate_half, up_half
     )
     deltas, partial_gram = backward_all(
-        every_residual.reshape(shape), slope, active, hidden, block, down_half
+        every_residual, slope, active, hidden, block, down_half
     )
     upper = jnp.sum(sum_everywhere(partial_gram), axis=1)
     order = [
@@ -373,6 +529,7 @@
     )
     out_specs = (P("client", "param"), P("client", "param"), P("client", "param"), P())
     shared = mesh.shape["client"] <= 8 and mesh.shape["client"] == PAIR * mesh.shape["param"]
+    shared = shared and mesh.shape["param"] == 4
     body = on_device_shared if shared else on_device
     return jax.shard_map(
         body, mesh=mesh, in_specs=in_specs, out_specs=out_specs, check_vma=False

time: 400 us -> 309 us (0.77)
  waiting for transfers between devices: 192 us -> 4.52 us
  Pallas kernels: 89.4 us -> 220 us
  local copies, waits for them, and re-layouts: 57.1 us -> 26.5 us
    all_gather x3 -> x0, waiting for transfers between devices: 151 us -> none  [the longest x1 57.5 us: on_device_shared(): every_input = lax.all_gather(inputs[0], ('client', 'param'), axis=0)]
    pallas_call x0 -> x2, Pallas kernels: none -> 130 us  [gather_everything(): pl.pallas_call(gather_kernel, in_specs=[pl.BlockSpec(memory_space=pl.ANY)...]
    all_gather x2 -> x0, local copies, waits for them, and re-layouts: 39.2 us -> none  [the longest x1 20.4 us: on_device_shared(): every_residual = lax.all_gather(local_residual, ('client', 'param'), axis=0)]
    reduce_scatter x1 -> x0, waiting for transfers between devices: 35 us -> none  [on_device_shared(): lax.psum_scatter(partial_out.astype(jnp.bfloat16), 'param', scatter_dimen...]
    dynamic_slice x1, local copies, waits for them, and re-layouts: 5.22 us -> 9.59 us  [on_device_shared(): up_half = lax.dynamic_slice_in_dim(up_weight, core * half, half, 1)]
  transfers between devices with their start and end apart: 5 -> 2, of which waited for: 5 -> 1; matrix products, arithmetic and copies ran while one was open for 8% -> 5% of each run, Pallas kernels for 8% -> 11%
where the time goes in v3:
time: 309 us; the launch traced here: 308 us
  Pallas kernels  220 us (71%)
  local copies, waits for them, and re-layouts  26.5 us (9%)
  other arithmetic  24.5 us (8%)
  matrix products  17.6 us (6%)
  between operations  14.9 us (5%)
  waiting for transfers between devices  4.52 us (1%)
    pallas_call x2, Pallas kernels, gather_everything(): pl.pallas_call(gather_kernel, in_specs=[pl.BlockSpec(memory_space=pl.ANY)...  130 us
    pallas_call x1, Pallas kernels, backward_all(): pl.pallas_call(backward_kernel, grid=(clients,), in_specs=[client_block((...  45.3 us
    pallas_call x1, Pallas kernels, forward_all(): pl.pallas_call(forward_kernel, grid=(clients,), in_specs=[client_block((p...  33.7 us
    reduce_sum x1, other arithmetic, on_device_shared(): jnp.sum(weights[None, :, None, None] * deltas.astype(jnp.float32), axis=1)  12.7 us
    dot_general x1, matrix products, on_device_shared(): jnp.dot(hidden, down_weight, preferred_element_type=jnp.float32)  11.4 us
    pallas_call x1, Pallas kernels, sum_everywhere(): pl.pallas_call(sum_kernel, in_specs=[pl.BlockSpec(memory_space=pltpu.VMEM...  10.9 us
    dynamic_slice x1, local copies, waits for them, and re-layouts, on_device_shared(): up_half = lax.dynamic_slice_in_dim(up_weight, core * half, half, 1)  9.59 us
    dot_general x1, matrix products, on_device_shared(): jnp.dot(normed_own, gate_weight, preferred_element_type=jnp.float32)  6.21 us
  transfers between devices with their start and end apart: 2, of which 1 were waited for; matrix products, arithmetic and copies ran while one was open for 5% of the time, Pallas kernels for 11%

profile of v3, /device:TPU:0, one launch (start us, length us, event | category | flops | bytes accessed | tf_op | source)
XLA Modules:
  0.0 308.3 jit_solution(8445760185635912927)
XLA Ops:
  7.2 0.0 reduce-scatter.4.cloned.1.call-start
  7.2 1.2 fusion.36
  8.4 0.2 copy.28
  8.6 0.2 copy.29
  8.8 0.9 pad_maximum_fusion.5.block_ref
  9.7 66.4 %gather_everything.2.rows_ref = bf16[8,4,192,1152]{3,2,1,0:T(8,128)(2,1)} custom-call(bf16[192,1152]{1,0:T(8,128)(2,1)} %pad_maximum_fusion.5.block_ref), custom_call_target="tpu_custom_call" | custom-call | tf_op jit(solution)/shard_map/gather_everything/pallas_call | solution.py:389
  76.1 1.6 dynamic-slice_bitcast_fusion.1
  77.7 0.3 fusion.32
  78.1 0.3 fusion.34
  78.4 0.8 pad_maximum_fusion.1
  79.2 2.5 concatenate.33
  81.7 0.4 fusion.1
  82.2 0.0 copy-done.2
  82.2 6.2 %fusion.21 = f32[384,1152]{1,0:T(8,128)} fusion(bf16[2304,1152]{1,0:T(8,128)(2,1)} %param.11, bf16[384,2304]{1,0:T(8,128)(2,1)S(1)} %concatenate.33, f32[2304]{0:T(1024)S(1)} %copy-done.2, f32[384]{0:T(512)S(1)} %add_rsqrt_fusion), kind=kOutput, calls=%fused_computation.36 | convolution fusion | flops 2041970688 | bytes 8858112 | tf_op jit(solution)/shard_map/dot_general | solution.py:484
  88.4 11.4 %fusion = bf16[2304,384]{1,0:T(8,128)(2,1)} fusion(bf16[1152,2304]{1,0:T(8,128)(2,1)} %param.13, bf16[2304,1152]{1,0:T(8,128)(2,1)} %param.12, f32[384,1152]{1,0:T(8,128)} %fusion.21, bf16[384,2304]{1,0:T(8,128)(2,1)S(1)} %concatenate.33, f32[2304]{0:T(1024)S(1)} %copy-done.2, f32[384]{0:T(512)S(1)} %add_rsqrt_fusion), kind=kOutput, calls=%fused_computation.10 | convolution fusion | flops 4085710848 | bytes 15936000 | tf_op jit(solution)/shard_map/dot_general | solution.py:487
  99.8 0.0 reduce-scatter.4.cloned.1.call-update
  99.8 0.7 reshape.44.gain_ref
  100.5 0.0 copy-done.1
  100.5 0.3 copy.24
  100.8 0.0 copy-done.3
  100.8 3.4 %constant_dynamic-slice_fusion.down_ref = bf16[576,2304]{1,0:T(8,128)(2,1)} fusion(bf16[1152,2304]{1,0:T(8,128)(2,1)} %param.13, s32[]{:T(128)S(6)} %select_n.69), kind=kLoop, calls=%fused_computation.54 | loop fusion | bytes 5308420 | tf_op jit(solution)/shard_map/dynamic_slice | solution.py:496
  104.2 9.6 %constant_dynamic-slice_fusion.1 = (bf16[2304,576]{1,0:T(8,128)(2,1)}, bf16[2304,576]{1,0:T(8,128)(2,1)}) fusion(bf16[2304,1152]{1,0:T(8,128)(2,1)} %param.12, s32[]{:T(128)S(6)} %select_n.69, bf16[2304,1152]{1,0:T(8,128)(2,1)} %param.11), kind=kLoop, calls=%fused_computation.55 | loop fusion | bytes 10616836 | tf_op jit(solution)/shard_map/dynamic_slice | solution.py:495
  113.8 33.7 %forward_all.1 = (f32[8,384,576]{2,1,0:T(8,128)}, f32[8,384,576]{2,1,0:T(8,128)}, bf16[8,384,576]{2,1,0:T(8,128)(2,1)}, bf16[8,384,576]{2,1,0:T(8,128)(2,1)}) custom-call(bf16[8,4,192,1152]{3,2,1,0:T(8,128)(2,1)} %gather_everything.2.rows_ref, f32[4,1,576]{2,1,0:T(1,128)} %reshape.44.gain_ref, bf16[2304,576]{1,0:T(8,128)(2,1)} %get-tuple-element.51.gate_ref, ...), custom_call_target="tpu_custom_call" | custom-call | flops 16307453952 | bytes 41943040 | tf_op jit(solution)/shard_map/forward_all/pallas_call | solution.py:132
  147.6 1.3 copy.27
  148.8 0.2 fusion.18
  149.0 0.9 pad_maximum_fusion.6.block_ref
  149.9 63.9 %gather_everything.3.rows_ref = bf16[8,4,192,1152]{3,2,1,0:T(8,128)(2,1)} custom-call(bf16[192,1152]{1,0:T(8,128)(2,1)} %pad_maximum_fusion.6.block_ref), custom_call_target="tpu_custom_call" | custom-call | tf_op jit(solution)/shard_map/gather_everything/pallas_call | solution.py:389
  213.8 45.3 %backward_all.1 = (bf16[3,8,576,576]{3,2,1,0:T(8,128)(2,1)}, f32[40,128]{1,0:T(8,128)}) custom-call(bf16[8,4,192,1152]{3,2,1,0:T(8,128)(2,1)} %gather_everything.3.rows_ref, f32[8,384,576]{2,1,0:T(8,128)} %get-tuple-element.12.slope_ref, f32[8,384,576]{2,1,0:T(8,128)} %get-tuple-element.13.active_ref, bf16[8,384,576]{2,1,0:T(8,128)(2,1)} %get-tuple-element.14.hidden_ref, ...), custom_call_target="tpu_custom_call" | custom-call | flops 14269022208 | bytes 52428800 | tf_op jit(solution)/shard_map/backward_all/pallas_call | solution.py:221
  259.1 10.9 %sum_everywhere.1 = f32[40,128]{1,0:T(8,128)} custom-call(f32[40,128]{1,0:T(8,128)} %get-tuple-element.16.part_ref), custom_call_target="tpu_custom_call" | custom-call | tf_op jit(solution)/shard_map/sum_everywhere/pallas_call | solution.py:447
  270.0 0.8 reduce_sum.55
  270.9 0.8 gather_fusion
  271.6 0.1 reshape.48
  271.7 0.1 copy.25
  271.8 0.6 gather_fusion.1
  272.4 0.1 subtract_select_fusion
  272.5 0.7 sort.15
  273.2 0.0 copy-done.4
  273.2 0.6 fusion.24
  274.4 0.6 fusion.30
  275.1 1.2 broadcast_multiply_fusion
  276.2 12.7 %multiply_reduce_fusion = f32[3,576,576]{2,1,0:T(8,128)S(1)} fusion(bf16[3,8,576,576]{3,2,1,0:T(8,128)(2,1)} %get-tuple-element.18, f32[8]{0:T(128)S(1)} %get-tuple-element.22), kind=kLoop, calls=%fused_computation.2 | loop fusion | flops 22892544 | bytes 19906592 | tf_op jit(solution)/shard_map/reduce_sum | solution.py:509
  288.9 0.0 copy-start
  288.9 2.0 copy-done
  290.9 1.5 dynamic-slice_bitcast_fusion
  292.5 0.0 collective-permute-start
  292.5 4.5 %collective-permute-done = f32[3,288,576]{2,1,0:T(8,128)S(1)} collective-permute-done((f32[3,288,576]{2,1,0:T(8,128)}, f32[3,288,576]{2,1,0:T(8,128)S(1)}, u32[]{:S(2)}, u32[]{:S(2)}) %collective-permute-start) | collective-permute-done | bytes 1990688 | tf_op jit(solution)/shard_map/ppermute | solution.py:513
  297.0 1.9 bitcast_select_fusion
  298.9 2.6 fusion.16
  (13 shorter events, 0.2 us)
Async XLA Ops:
  7.2 140.4 %reduce-scatter.4.cloned.1.call-start = ((), (), s32[]{:S(2)}) async-start(), calls=%async_computation.1 | async-start | bytes 2211840
  79.2 2.9 copy-start.2
  88.4 12.1 %copy-start.1 = (bf16[1,384,576]{1,2,0:T(8,128)(2,1)S(1)}, bf16[1,384,576]{1,2,0:T(8,128)(2,1)}, u32[]{:S(2)}) copy-start(bf16[1,384,576]{1,2,0:T(8,128)(2,1)} %param.9) | copy-start | bytes 1327108
  99.8 1.0 copy-start.3
  259.1 14.1 %copy-start.4 = (s32[8]{0:T(128)S(1)}, s32[8]{0:T(128)}, u32[]{:S(2)}) copy-start(s32[8]{0:T(128)} %param.14) | copy-start | bytes 100
  288.9 2.0 copy-start
  292.5 4.5 %collective-permute-start = (f32[3,288,576]{2,1,0:T(8,128)}, f32[3,288,576]{2,1,0:T(8,128)S(1)}, u32[]{:S(2)}, u32[]{:S(2)}) collective-permute-start(f32[3,288,576]{2,1,0:T(8,128)} %dynamic-slice_bitcast_fusion), channel_id=1, source_target_pairs={{0,4},{4,0},{8,12},{12,8},{16,20},{20,16},{24,28},{28,24},{1,5},{5... | collective-permute-start | bytes 5971976 | tf_op jit(solution)/shard_map/ppermute | solution.py:513
Sparse Core Ops, SparseCore 0:
  99.9 31.6 reduce-scatter.3

commit v4 on v3

--- a/solution.py
+++ b/solution.py
@@ -102,10 +102,19 @@
 
 
 def forward_kernel(
-    rows_ref, gain_ref, gate_ref, up_ref, slope_ref, active_ref, hidden_ref, block_ref, normed
+    rows_ref, gain_ref, gate_ref, up_ref, slope_ref, active_ref, hidden_ref, block_ref, normed,
+    gate_half, up_half,
 ):
     params, width = rows_ref.shape[0], rows_ref.shape[2] // 2
     chip = lax.axis_index("client") // PAIR
+    half = gate_half.shape[1]
+    for side in range(PAIR):
+
+        @pl.when((pl.program_id(0) == 0) & (lax.rem(lax.axis_index("client"), PAIR) == side))
+        def _(side=side):
+            gate_half[...] = gate_ref[:, side * half : (side + 1) * half]
+            up_half[...] = up_ref[:, side * half : (side + 1) * half]
+
     total = 0.0
     for at in range(params):
         wide = unpacked(rows_ref[at]).astype(jnp.float32)
@@ -115,18 +124,18 @@
         wide = unpacked(rows_ref[at]).astype(jnp.float32)
         normed[:, at * width : (at + 1) * width] = (wide * inverse * gain_ref[at]).astype(jnp.bfloat16)
     block_ref[...] = (unpacked(rows_ref[chip]).astype(jnp.float32) * inverse * gain_ref[chip]).astype(jnp.bfloat16)
-    gate = jnp.dot(normed[...], gate_ref[...], preferred_element_type=jnp.float32)
-    up = jnp.dot(normed[...], up_ref[...], preferred_element_type=jnp.float32)
+    gate = jnp.dot(normed[...], gate_half[...], preferred_element_type=jnp.float32)
+    up = jnp.dot(normed[...], up_half[...], preferred_element_type=jnp.float32)
     active, slope = gelu_parts(gate)
     slope_ref[...] = slope * up
     active_ref[...] = active
     hidden_ref[...] = (active * up).astype(jnp.bfloat16)
 
 
-def forward_all(every_input, norm_gain, gate_half, up_half):
+def forward_all(every_input, norm_gain, gate_weight, up_weight):
     clients, params, rows, lanes = every_input.shape
     tokens, width = 2 * rows, lanes // 2
-    depth, half = gate_half.shape
+    depth, half = gate_weight.shape[0], gate_weight.shape[1] // PAIR
     client_block = lambda shape: pl.BlockSpec((None,) + shape, lambda at: (at,) + (0,) * len(shape))
     whole = lambda shape: pl.BlockSpec(shape, lambda at: (0,) * len(shape))
     return pl.pallas_call(
@@ -135,8 +144,8 @@
         in_specs=[
             client_block((params, rows, lanes)),
             whole((params, 1, width)),
-            whole((depth, half)),
-            whole((depth, half)),
+            pl.BlockSpec(memory_space=pltpu.VMEM),
+            pl.BlockSpec(memory_space=pltpu.VMEM),
         ],
         out_specs=[client_block((tokens, half))] * 3 + [client_block((tokens, width))],
         out_shape=[
@@ -145,13 +154,17 @@
             jax.ShapeDtypeStruct((clients, tokens, half), jnp.bfloat16),
             jax.ShapeDtypeStruct((clients, tokens, width), jnp.bfloat16),
         ],
-        scratch_shapes=[pltpu.VMEM((tokens, depth), jnp.bfloat16)],
+        scratch_shapes=[
+            pltpu.VMEM((tokens, depth), jnp.bfloat16),
+            pltpu.VMEM((depth, half), jnp.bfloat16),
+            pltpu.VMEM((depth, half), jnp.bfloat16),
+        ],
         compiler_params=pltpu.CompilerParams(vmem_limit_bytes=56 * 2**20),
         cost_estimate=pl.CostEstimate(
             flops=4 * clients * tokens * depth * half, bytes_accessed=40 * 2**20, transcendentals=0
         ),
         name="forward_all",
-    )(every_input, norm_gain.reshape(params, 1, width), gate_half, up_half)
+    )(every_input, norm_gain.reshape(params, 1, width), gate_weight, up_weight)
 
 
 def backward_kernel(
@@ -164,8 +177,9 @@
     chip = lax.axis_index("client") // PAIR
     for at in range(params):
         residual[:, at * width : (at + 1) * width] = unpacked(rows_ref[at])
+    first = pl.multiple_of(lax.rem(lax.axis_index("client"), PAIR) * columns, columns)
     back = lax.dot_general(
-        residual[...], down_ref[...], (((1,), (1,)), ((), ())), preferred_element_type=jnp.float32
+        residual[...], down_ref[pl.ds(first, columns), :], (((1,), (1,)), ((), ())), preferred_element_type=jnp.float32
     )
     back_gate = (back * slope_ref[...]).astype(jnp.bfloat16)
     back_up = (back * active_ref[...]).astype(jnp.bfloat16)
@@ -211,10 +225,10 @@
         gram_ref[: len(pairs), :] = jnp.sum(totals[...], axis=1)
 
 
-def backward_all(every_residual, slope, active, hidden, block, down_half):
+def backward_all(every_residual, slope, active, hidden, block, down_weight):
     clients, params, packed_rows, lanes = every_residual.shape
     tokens, width = 2 * packed_rows, lanes // 2
-    half, depth = down_half.shape
+    half, depth = down_weight.shape[0] // PAIR, down_weight.shape[1]
     pair_count = clients * (clients + 1) // 2
     padded = -(-pair_count // 8) * 8
     client_block = lambda shape: pl.BlockSpec((None,) + shape, lambda at: (at,) + (0,) * len(shape))
@@ -223,7 +237,7 @@
         grid=(clients,),
         in_specs=[client_block((params, packed_rows, lanes))]
         + [client_block((tokens, half))] * 3
-        + [client_block((tokens, width)), pl.BlockSpec((half, depth), lambda at: (0, 0))],
+        + [client_block((tokens, width)), pl.BlockSpec(memory_space=pltpu.VMEM)],
         out_specs=[
             pl.BlockSpec((3, None, width, half), lambda at: (0, at, 0, 0)),
             pl.BlockSpec((padded, 128), lambda at: (0, 0)),
@@ -244,7 +258,7 @@
             transcendentals=0,
         ),
         name="backward_all",
-    )(every_residual, slope, active, hidden, block, down_half)
+    )(every_residual, slope, active, hidden, block, down_weight)
 
 
 COLUMN, ACROSS, ALONG, FIRST, SECOND, SHARED, DOWN = 0, 1, 2, 3, 4, 5, 10
@@ -399,6 +413,42 @@
         compiler_params=pltpu.CompilerParams(collective_id=1, has_side_effects=True),
         name="gather_everything",
     )(block)
+
+
+def weighted_kernel(weight_ref, delta_ref, kept_ref, sent_ref):
+    clients, rows, _ = delta_ref.shape
+    core = lax.rem(lax.axis_index("client"), PAIR)
+    height = rows // PAIR
+    for side, out_ref in ((core, kept_ref), (1 - core, sent_ref)):
+
+        def step(index, carry, side=side, out_ref=out_ref):
+            row = pl.multiple_of(index * 16, 16)
+            from_row = pl.multiple_of(side * height + index * 16, 16)
+            total = weight_ref[0] * delta_ref[0, pl.ds(from_row, 16), :].astype(jnp.float32)
+            for client in range(1, clients):
+                tile = delta_ref[client, pl.ds(from_row, 16), :].astype(jnp.float32)
+                total = total + weight_ref[client] * tile
+            out_ref[pl.ds(row, 16), :] = total
+            return carry
+
+        lax.fori_loop(0, height // 16, step, 0, unroll=2)
+
+
+def weighted_halves(weights, deltas):
+    kinds, clients, rows, half = deltas.shape
+    shape = jax.ShapeDtypeStruct((kinds, rows // PAIR, half), jnp.float32)
+    return pl.pallas_call(
+        weighted_kernel,
+        grid=(kinds,),
+        in_specs=[
+            pl.BlockSpec(memory_space=pltpu.SMEM),
+            pl.BlockSpec((None, clients, rows, half), lambda kind: (kind, 0, 0, 0)),
+        ],
+        out_specs=[pl.BlockSpec((None, rows // PAIR, half), lambda kind: (kind, 0, 0))] * 2,
+        out_shape=[shape, shape],
+        compiler_params=pltpu.CompilerParams(vmem_limit_bytes=40 * 2**20),
+        name="weighted_halves",
+    )(weights, deltas)
 
 
 def sum_kernel(part_ref, total_ref, params_held, clients_held, summed, sends, receives):
@@ -491,14 +541,11 @@
     local_residual = ((out_share - targets[0].astype(jnp.float32)) * factor).astype(jnp.bfloat16)
     every_residual = gather_everything(packed(local_residual))
 
-    gate_half = lax.dynamic_slice_in_dim(gate_weight, core * half, half, 1)
-    up_half = lax.dynamic_slice_in_dim(up_weight, core * half, half, 1)
-    down_half = lax.dynamic_slice_in_dim(down_weight, core * half, half, 0)
     slope, active, hidden, block = forward_all(
-        every_input, norm_gain, gate_half, up_half
+        every_input, norm_gain, gate_weight, up_weight
     )
     deltas, partial_gram = backward_all(
-        every_residual, slope, active, hidden, block, down_half
+        every_residual, slope, active, hidden, block, down_weight
     )
     upper = jnp.sum(sum_everywhere(partial_gram), axis=1)
     order = [
@@ -506,10 +553,7 @@
     ]
     gram = upper[jnp.asarray(order)]
     weights = krum_weights(gram, neighbours)
-    updates = jnp.sum(weights[None, :, None, None] * deltas.astype(jnp.float32), axis=1)
-    updates = updates.reshape(3, PAIR, chip_rows // PAIR, half)
-    kept = lax.dynamic_index_in_dim(updates, core, 1, keepdims=False)
-    sent = lax.dynamic_index_in_dim(updates, 1 - core, 1, keepdims=False)
+    kept, sent = weighted_halves(weights, deltas)
     arrived = lax.ppermute(sent, "client", [(i, i ^ 1) for i in range(clients)])
     first = jnp.where(core == 0, kept, arrived)
     second = jnp.where(core == 0, arrived, kept)

time: 309 us -> 294 us (0.951)
  local copies, waits for them, and re-layouts: 26.5 us -> 9.97 us
  Pallas kernels: 220 us -> 234 us
  other arithmetic: 24.5 us -> 11.8 us
    dynamic_slice x2 -> x0, local copies, waits for them, and re-layouts: 13 us -> none  [the longest x1 9.59 us: on_device_shared(): up_half = lax.dynamic_slice_in_dim(up_weight, core * half, half, 1)]
    reduce_sum x1 -> x0, other arithmetic: 12.7 us -> none  [on_device_shared(): jnp.sum(weights[None, :, None, None] * deltas.astype(jnp.float32), axis=1)]
    pallas_call x0 -> x1, Pallas kernels: none -> 9.46 us  [weighted_halves(): pl.pallas_call(weighted_kernel, grid=(kinds,), in_specs=[pl.BlockSpec(mem...]
  transfers between devices with their start and end apart: 2 -> 2, of which waited for: 1 -> 1; matrix products, arithmetic and copies ran while one was open for 5% -> 0% of each run, Pallas kernels for 11% -> 12%
where the time goes in v4:
time: 294 us; the launch traced here: 293 us
  Pallas kernels  234 us (80%)
  matrix products  17.6 us (6%)
  between operations  14.8 us (5%)
  other arithmetic  11.8 us (4%)
  local copies, waits for them, and re-layouts  9.97 us (3%)
  waiting for transfers between devices  4.31 us (1%)
    pallas_call x2, Pallas kernels, gather_everything(): pl.pallas_call(gather_kernel, in_specs=[pl.BlockSpec(memory_space=pl.ANY)...  132 us
    pallas_call x1, Pallas kernels, backward_all(): pl.pallas_call(backward_kernel, grid=(clients,), in_specs=[client_block((...  46.1 us
    pallas_call x1, Pallas kernels, forward_all(): pl.pallas_call(forward_kernel, grid=(clients,), in_specs=[client_block((p...  35.4 us
    dot_general x1, matrix products, on_device_shared(): jnp.dot(hidden, down_weight, preferred_element_type=jnp.float32)  11.4 us
    pallas_call x1, Pallas kernels, sum_everywhere(): pl.pallas_call(sum_kernel, in_specs=[pl.BlockSpec(memory_space=pltpu.VMEM...  10.6 us
    pallas_call x1, Pallas kernels, weighted_halves(): pl.pallas_call(weighted_kernel, grid=(kinds,), in_specs=[pl.BlockSpec(mem...  9.46 us
    dot_general x1, matrix products, on_device_shared(): jnp.dot(normed_own, gate_weight, preferred_element_type=jnp.float32)  6.24 us
  transfers between devices with their start and end apart: 2, of which 1 were waited for; matrix products, arithmetic and copies ran while one was open for 0% of the time, Pallas kernels for 12%

profile of v4, /device:TPU:0, one launch (start us, length us, event | category | flops | bytes accessed | tf_op | source)
XLA Modules:
  0.0 293.0 jit_solution(9955911906699285577)
XLA Ops:
  7.2 0.0 reduce-scatter.4.cloned.1.call-start
  7.2 1.2 fusion.36
  8.4 0.2 copy.28
  8.6 0.2 copy.29
  8.8 0.9 pad_maximum_fusion.5.block_ref
  9.7 66.4 %gather_everything.2.rows_ref = bf16[8,4,192,1152]{3,2,1,0:T(8,128)(2,1)} custom-call(bf16[192,1152]{1,0:T(8,128)(2,1)} %pad_maximum_fusion.5.block_ref), custom_call_target="tpu_custom_call" | custom-call | tf_op jit(solution)/shard_map/gather_everything/pallas_call | solution.py:403
  76.1 1.6 dynamic-slice_bitcast_fusion
  77.7 0.3 fusion.32
  78.1 0.3 fusion.34
  78.4 0.8 pad_maximum_fusion.1
  79.2 0.0 copy-start.1
  79.2 2.5 concatenate.33
  81.7 0.4 fusion.1
  82.2 0.0 copy-done.1
  82.2 6.2 %fusion.21 = f32[384,1152]{1,0:T(8,128)} fusion(bf16[2304,1152]{1,0:T(8,128)(2,1)} %gate_ref.1, bf16[384,2304]{1,0:T(8,128)(2,1)S(1)} %concatenate.33, f32[2304]{0:T(1024)S(1)} %copy-done.1, f32[384]{0:T(512)S(1)} %add_rsqrt_fusion), kind=kOutput, calls=%fused_computation.34 | convolution fusion | flops 2041970688 | bytes 8858112 | tf_op jit(solution)/shard_map/dot_general | solution.py:534
  88.4 0.0 copy-start
  88.4 11.4 %fusion = bf16[2304,384]{1,0:T(8,128)(2,1)} fusion(bf16[1152,2304]{1,0:T(8,128)(2,1)} %down_ref.1, bf16[2304,1152]{1,0:T(8,128)(2,1)} %up_ref.1, f32[384,1152]{1,0:T(8,128)} %fusion.21, bf16[384,2304]{1,0:T(8,128)(2,1)S(1)} %concatenate.33, f32[2304]{0:T(1024)S(1)} %copy-done.1, f32[384]{0:T(512)S(1)} %add_rsqrt_fusion), kind=kOutput, calls=%fused_computation.9 | convolution fusion | flops 4085710848 | bytes 15936000 | tf_op jit(solution)/shard_map/dot_general | solution.py:537
  99.8 0.0 copy-start.2
  99.8 0.0 reduce-scatter.4.cloned.1.call-update
  99.8 0.7 reshape.35.gain_ref
  100.5 0.0 copy-done
  100.5 0.3 copy.24
  100.8 0.0 copy-done.2
  100.8 35.4 %forward_all.1 = (f32[8,384,576]{2,1,0:T(8,128)}, f32[8,384,576]{2,1,0:T(8,128)}, bf16[8,384,576]{2,1,0:T(8,128)(2,1)}, bf16[8,384,576]{2,1,0:T(8,128)(2,1)}) custom-call(bf16[8,4,192,1152]{3,2,1,0:T(8,128)(2,1)} %gather_everything.2.rows_ref, f32[4,1,576]{2,1,0:T(1,128)} %reshape.35.gain_ref, bf16[2304,1152]{1,0:T(8,128)(2,1)} %gate_ref.1, ...), custom_call_target="tpu_custom_call" | custom-call | flops 16307453952 | bytes 41943040 | tf_op jit(solution)/shard_map/forward_all/pallas_call | solution.py:141
  136.2 0.0 reduce-scatter.4.cloned.1.call-done
  136.2 1.3 copy.27
  137.5 0.2 fusion.18
  137.7 0.9 pad_maximum_fusion.6.block_ref
  138.6 65.9 %gather_everything.3.rows_ref = bf16[8,4,192,1152]{3,2,1,0:T(8,128)(2,1)} custom-call(bf16[192,1152]{1,0:T(8,128)(2,1)} %pad_maximum_fusion.6.block_ref), custom_call_target="tpu_custom_call" | custom-call | tf_op jit(solution)/shard_map/gather_everything/pallas_call | solution.py:403
  204.5 46.1 %backward_all.1 = (bf16[3,8,576,576]{3,2,1,0:T(8,128)(2,1)}, f32[40,128]{1,0:T(8,128)}) custom-call(bf16[8,4,192,1152]{3,2,1,0:T(8,128)(2,1)} %gather_everything.3.rows_ref, f32[8,384,576]{2,1,0:T(8,128)} %get-tuple-element.14.slope_ref, f32[8,384,576]{2,1,0:T(8,128)} %get-tuple-element.15.active_ref, bf16[8,384,576]{2,1,0:T(8,128)(2,1)} %get-tuple-element.16.hidden_ref, ...), custom_call_target="tpu_custom_call" | custom-call | flops 14269022208 | bytes 52428800 | tf_op jit(solution)/shard_map/backward_all/pallas_call | solution.py:235
  250.6 10.6 %sum_everywhere.1 = f32[40,128]{1,0:T(8,128)} custom-call(f32[40,128]{1,0:T(8,128)} %get-tuple-element.18.part_ref), custom_call_target="tpu_custom_call" | custom-call | tf_op jit(solution)/shard_map/sum_everywhere/pallas_call | solution.py:497
  261.2 0.8 reduce_sum.46
  262.0 0.0 copy-start.3
  262.0 0.8 gather_fusion
  262.8 0.1 reshape.38
  262.9 0.1 copy.25
  262.9 0.6 gather_fusion.1
  263.6 0.1 subtract_select_fusion
  263.7 0.7 sort.15
  264.3 0.0 copy-done.3
  264.3 0.6 fusion.24
  265.6 0.6 fusion.30
  266.2 1.2 broadcast_multiply_fusion
  267.4 9.5 %weighted_halves.1 = (f32[3,288,576]{2,1,0:T(8,128)S(1)}, f32[3,288,576]{2,1,0:T(8,128)}) custom-call(f32[8]{0:T(128)S(1)} %get-tuple-element.26.weight_ref, bf16[3,8,576,576]{3,2,1,0:T(8,128)(2,1)} %get-tuple-element.20.delta_ref), custom_call_target="tpu_custom_call" | custom-call | tf_op jit(solution)/shard_map/weighted_halves/pallas_call | solution.py:440
  276.8 0.6 collective-permute-start
  277.4 4.3 %collective-permute-done = f32[3,288,576]{2,1,0:T(8,128)} collective-permute-done((f32[3,288,576]{2,1,0:T(8,128)}, f32[3,288,576]{2,1,0:T(8,128)}, u32[]{:S(2)}, u32[]{:S(2)}) %collective-permute-start) | collective-permute-done | bytes 1990688 | tf_op jit(solution)/shard_map/ppermute | solution.py:557
  281.7 1.9 broadcast_select_fusion
  283.6 2.6 fusion.16
  (8 shorter events, 0.2 us)
Async XLA Ops:
  7.2 129.0 %reduce-scatter.4.cloned.1.call-start = ((), (), s32[]{:S(2)}) async-start(), calls=%async_computation.1 | async-start | bytes 2211840
  79.2 2.9 %copy-start.1 = (f32[2304]{0:T(1024)S(1)}, f32[2304]{0:T(1024)}, u32[]{:S(2)}) copy-start(f32[2304]{0:T(1024)} %param.10) | copy-start | bytes 27652
  88.4 12.1 %copy-start = (bf16[1,384,576]{1,2,0:T(8,128)(2,1)S(1)}, bf16[1,384,576]{1,2,0:T(8,128)(2,1)}, u32[]{:S(2)}) copy-start(bf16[1,384,576]{1,2,0:T(8,128)(2,1)} %param.9) | copy-start | bytes 1327108
  99.8 1.0 copy-start.2
  262.0 2.3 copy-start.3
  276.8 4.9 %collective-permute-start = (f32[3,288,576]{2,1,0:T(8,128)}, f32[3,288,576]{2,1,0:T(8,128)}, u32[]{:S(2)}, u32[]{:S(2)}) collective-permute-start(f32[3,288,576]{2,1,0:T(8,128)} %get-tuple-element.22), channel_id=1, source_target_pairs={{0,4},{4,0},{8,12},{12,8},{16,20},{20,16},{24,28},{28,24},{1,5},{5... | collective-permute-start | bytes 5971976 | tf_op jit(solution)/shard_map/ppermute | solution.py:557
Sparse Core Ops, SparseCore 0:
  100.0 31.6 reduce-scatter.3
